TPU v7x, 512 devices: a whole 4x8x8 slice. The times are simulated.
512 devices in a mesh: row: 64 (over z, x, core), col: 8 (over y).
Axes of the slice: x: 4, y: 8, z: 8, core: 2. Of those that a mesh axis runs over, the one named last changes fastest.
Arguments:
- features: bfloat16 [512, 256, 384], P('row', 'col'), may hold values from -6 to 6
- depth_weight: float32 [7, 7, 384], replicated, may hold values from -0.875 to 0.875
- depth_bias: float32 [384], replicated, may hold values from -3 to 3
- norm_gain: float32 [384], replicated, may hold values from 0.25 to 1.75
- norm_bias: float32 [384], replicated, may hold values from -2 to 2
- expand_weight: bfloat16 [384, 1536], replicated, may hold values from -0.3125 to 0.3125
- expand_bias: float32 [1536], replicated, may hold values from -3 to 3
- shrink_weight: bfloat16 [1536, 384], replicated, may hold values from -0.15625 to 0.15625
- shrink_bias: float32 [384], replicated, may hold values from -3 to 3
- layer_scale: float32 [384], replicated, may hold values from 0.3 to 3
- key_weight: bfloat16 [384, 384], replicated, may hold values from -0.3125 to 0.3125
- value_weight: bfloat16 [384, 384], replicated, may hold values from -0.3125 to 0.3125
- queries: bfloat16 [64, 384], replicated, may hold values from -192 to 192
- class_weight: float32 [384, 16], replicated, may hold values from -0.109375 to 0.109375
- tissue: int32 [64, 32], P('row', 'col'), may hold values from 0 to 1, as said below
- slide_label: int32 [16], replicated, may hold values from 0 to 1
Outputs:
- block_out: bfloat16 [512, 256, 384], P('row', 'col')
- pooled: float32 [64, 384], replicated
- slide_loss: float32 [1], replicated
Inputs may be any that keep to these rules, and one draw needn't show every extreme that they name: 0 or 1; tissue[0, 0] is 1.
All inputs are finite; a program needn't handle non-finite values.
Results may differ from a plain program's by a relative error of at most 0.028.
The roundings to bfloat16 on the way count: a program that leaves them out, or rounds other values in their place, can miss the bound.
Values may be sent and summed in bfloat16 or wider, within the bound.
No kernel may reach another device: no remote copies, remote signals or barrier semaphores. Data moves between devices by JAX's collectives and lax.ppermute only.
A program may use at most 128 MiB of HBM per device.

v0:
```python
import jax
import jax.numpy as jnp
from jax import lax
from jax.sharding import PartitionSpec as P

NH = 8
NQ = 64
TILE = 8
LOG2E = 1.4426950408889634
NEAR = [[z * 8 + r for r in range(8)] for z in range(8)]
FAR = [[z * 8 + r for z in range(8)] for r in range(8)]


def with_halo(block, sides, width):
    for axis, dim in sides:
        count = lax.axis_size(axis)
        forward = [(i, i + 1) for i in range(count - 1)]
        backward = [(target, source) for source, target in forward]
        low = lax.ppermute(
            lax.slice_in_dim(block, block.shape[dim] - width, None, axis=dim), axis, forward
        )
        high = lax.ppermute(lax.slice_in_dim(block, 0, width, axis=dim), axis, backward)
        block = jnp.concatenate([low, block, high], axis=dim)
    return block


def head_spread(width):
    size = width // NH
    head = lax.broadcasted_iota(jnp.int32, (NH, width), 0)
    channel = lax.broadcasted_iota(jnp.int32, (NH, width), 1)
    return (channel // size == head).astype(jnp.bfloat16)


def combined(parts, width):
    exponent = parts[:, :, width : width + NH]
    total = parts[:, :, width + NH : width + 2 * NH]
    top = jnp.max(exponent, axis=0)
    factor = jnp.exp2(exponent - top)
    total = jnp.sum(total * factor, axis=0)
    n, q = factor.shape[:2]
    spread = jnp.dot(
        factor.reshape(n * q, NH).astype(jnp.bfloat16),
        head_spread(width),
        preferred_element_type=jnp.float32,
    ).reshape(n, q, width)
    weighted = jnp.sum(parts[:, :, :width] * spread, axis=0)
    return weighted, top, total


def packed(weighted, top, total):
    q = weighted.shape[0]
    return jnp.concatenate(
        [weighted, top, total, jnp.zeros((q, 128 - 2 * NH), jnp.float32)], axis=1
    )


def everyone(part, axis, groups=None):
    return lax.all_to_all(
        jnp.broadcast_to(part[None], (8,) + part.shape), axis, 0, 0, axis_index_groups=groups, tiled=True
    )


def merged(weighted, top, total):
    width = weighted.shape[1]
    rows = packed(weighted, top, total).reshape(8, NQ // 8, width + 128)
    share = lax.all_to_all(rows, "row", 0, 0, axis_index_groups=NEAR, tiled=True)
    part = packed(*combined(share, width))
    part = packed(*combined(everyone(part, "row", FAR), width))
    weighted, top, total = combined(everyone(part, "col"), width)
    inverse = jnp.dot(
        1.0 / total, head_spread(width).astype(jnp.float32), precision=lax.Precision.HIGHEST
    )
    pooled = everyone(weighted * inverse, "row", NEAR)
    return pooled.reshape(NQ, width)


def per_device(
    features,
    depth_weight,
    depth_bias,
    norm_gain,
    norm_bias,
    expand_weight,
    expand_bias,
    shrink_weight,
    shrink_bias,
    layer_scale,
    key_weight,
    value_weight,
    queries,
    class_weight,
    tissue,
    slide_label,
):
    rows, cols, width = features.shape
    padded = with_halo(features, (("row", 0), ("col", 1)), 3)
    conv = jnp.zeros((rows, cols, width), jnp.float32) + depth_bias
    for offset_row in range(7):
        for offset_col in range(7):
            conv = (
                conv
                + padded[offset_row : offset_row + rows, offset_col : offset_col + cols].astype(
                    jnp.float32
                )
                * depth_weight[offset_row, offset_col]
            )
    center = jnp.mean(conv, axis=-1, keepdims=True)
    variance = jnp.mean((conv - center) ** 2, axis=-1, keepdims=True)
    normed = ((conv - center) * lax.rsqrt(variance + 1e-06) * norm_gain + norm_bias).astype(
        jnp.bfloat16
    )
    count = rows * cols
    expanded = (
        jnp.dot(normed.reshape(count, width), expand_weight, preferred_element_type=jnp.float32)
        + expand_bias
    )
    hidden = jax.nn.gelu(expanded, approximate=False).astype(jnp.bfloat16)
    shrunk = jnp.dot(hidden, shrink_weight, preferred_element_type=jnp.float32) + shrink_bias
    block_flat = (features.reshape(count, width).astype(jnp.float32) + layer_scale * shrunk).astype(
        jnp.bfloat16
    )
    keys = jnp.dot(block_flat, key_weight, preferred_element_type=jnp.float32).astype(jnp.bfloat16)
    values = jnp.dot(block_flat, value_weight, preferred_element_type=jnp.float32).astype(
        jnp.bfloat16
    )
    live_cells = jnp.repeat(jnp.repeat(tissue, TILE, axis=0), TILE, axis=1).reshape(count) > 0
    size = width // NH
    scores = jnp.einsum(
        "qhd,nhd->hqn",
        queries.reshape(NQ, NH, size),
        keys.reshape(count, NH, size),
        preferred_element_type=jnp.float32,
    ) * (size ** (-0.5) * LOG2E)
    live = live_cells[None, None, :]
    scores = jnp.where(live, scores, -1e30)
    top = jnp.ceil(jnp.max(scores, axis=2))
    weights = jnp.where(live, jnp.exp2(scores - top[:, :, None]), 0.0)
    total = jnp.sum(weights, axis=2)
    rounded = weights.astype(jnp.bfloat16)
    weighted = jnp.einsum(
        "hqn,nhd->qhd", rounded, values.reshape(count, NH, size), preferred_element_type=jnp.float32
    ).reshape(NQ, width)
    pooled = merged(weighted, top.T, total.T)
    logits = jnp.sum(jnp.dot(pooled, class_weight, precision=lax.Precision.HIGHEST), axis=0)
    slide_loss = jnp.sum(
        jax.nn.softplus(logits) - slide_label.astype(jnp.float32) * logits
    ).reshape(1)
    return (block_flat.reshape(rows, cols, width), pooled, slide_loss)


def solution(mesh):
    placed = (P("row", "col", None),) + (P(),) * 13 + (P("row", "col"), P())
    return jax.shard_map(
        per_device,
        mesh=mesh,
        in_specs=placed,
        out_specs=(P("row", "col", None), P(), P()),
        check_vma=False,
    )
```

profile of v0, /device:TPU:1, one launch (start us, length us, event | category | flops | bytes accessed | tf_op | source)
XLA Modules:
  0.0 93.8 jit_solution(13942997016295749400)
XLA Ops:
  0.6 0.0 copy-start
  0.6 0.0 copy-start.1
  0.7 1.0 %fusion.163 = (bf16[3,32,384]{2,1,0:T(8,128)(2,1)S(1)}, bf16[3,32,384]{2,1,0:T(8,128)(2,1)S(1)}) fusion(bf16[8,32,384]{2,1,0:T(8,128)(2,1)} %param.16), kind=kLoop, calls=%fused_computation.340 | loop fusion | bytes 294912 | tf_op jit(solution)/shard_map/slice | solution.py:22
  1.7 4.5 %collective-permute-start = (bf16[3,32,384]{2,1,0:T(8,128)(2,1)S(1)}, bf16[3,32,384]{2,1,0:T(8,128)(2,1)S(1)}, u32[]{:S(2)}, u32[]{:S(2)}) collective-permute-start(bf16[3,32,384]{2,1,0:T(8,128)(2,1)S(1)} %get-tuple-element.60), channel_id=1, source_target_pairs={{0,8},{8,16},{16,24},{24,32},{32,40},{40,48},{48,56},{56,64},{64,7... | collective-permute-start | bytes 221192 | tf_op jit(solution)/shard_map/ppermute | solution.py:19
  6.2 5.6 %collective-permute-start.1 = (bf16[3,32,384]{2,1,0:T(8,128)(2,1)S(1)}, bf16[3,32,384]{2,1,0:T(8,128)(2,1)S(1)}, u32[]{:S(2)}, u32[]{:S(2)}) collective-permute-start(bf16[3,32,384]{2,1,0:T(8,128)(2,1)S(1)} %get-tuple-element.59), channel_id=1, source_target_pairs={{8,0},{16,8},{24,16},{32,24},{40,32},{48,40},{56,48},{64,56},{72,6... | collective-permute-start | bytes 221192 | tf_op jit(solution)/shard_map/ppermute | solution.py:22
  11.8 1.1 %slice_reduce_fusion.50 = (f32[384]{0:T(512)S(1)}, f32[384]{0:T(512)S(1)}, f32[384]{0:T(512)S(1)}, f32[384]{0:T(512)S(1)}, f32[384]{0:T(512)S(1)}, /*index=5*/f3...) fusion(f32[7,7,384]{2,1,0:T(8,128)} %param.17), kind=kLoop, calls=%fused_computation.296 | loop fusion | bytes 58368 | tf_op jit(solution)/shard_map/slice | solution.py:105
  12.9 0.7 compare_bitcast_fusion
  13.6 1.3 %slice_reduce_fusion.51 = (f32[384]{0:T(512)S(1)}, f32[384]{0:T(512)S(1)}, f32[384]{0:T(512)S(1)}, f32[384]{0:T(512)S(1)}, f32[384]{0:T(512)S(1)}, /*index=5*/f3...) fusion(f32[7,7,384]{2,1,0:T(8,128)} %param.17), kind=kLoop, calls=%fused_computation.297 | loop fusion | bytes 58368 | tf_op jit(solution)/shard_map/slice | solution.py:105
  14.9 0.0 collective-permute-done
  14.9 1.0 %constant_dynamic-update-slice_fusion.3 = (bf16[11,32,384]{2,1,0:T(8,128)(2,1)S(1)}, bf16[14,32,384]{2,1,0:T(8,128)(2,1)S(1)}, bf16[11,32,384]{2,1,0:T(8,128)(2,1)S(1)}) fusion(bf16[11,32,384]{2,1,0:T(8,128)(2,1)S(1)} %get-tuple-element.61, bf16[8,32,384]{2,1,0:T(8,128)(2,1)} %param.16, bf16[14,32,384]{2,1,0:T(8,128)(2,1)S(1)} %get-tuple-element.62), kind=kLoop, calls=%fused_computation.220 | loop fusion | bytes 786432 | tf_op jit(solution)/shard_map/concatenate | solution.py:23
  15.9 0.0 collective-permute-done.1
  16.0 1.3 %collective-permute-start.3 = (bf16[14,3,384]{2,1,0:T(4,128)(2,1)S(1)}, bf16[14,3,384]{2,1,0:T(4,128)(2,1)S(1)}, u32[]{:S(2)}, u32[]{:S(2)}) collective-permute-start(bf16[14,3,384]{2,1,0:T(4,128)(2,1)S(1)} %get-tuple-element.55), channel_id=1, source_target_pairs={{1,0},{2,1},{3,2},{4,3},{5,4},{6,5},{7,6},{9,8},{10,9},{11,10},{12... | collective-permute-start | bytes 96776 | tf_op jit(solution)/shard_map/ppermute | solution.py:22
  17.3 4.0 %collective-permute-start.2 = (bf16[14,3,384]{2,1,0:T(4,128)(2,1)S(1)}, bf16[14,3,384]{2,1,0:T(4,128)(2,1)S(1)}, u32[]{:S(2)}, u32[]{:S(2)}) collective-permute-start(bf16[14,3,384]{2,1,0:T(4,128)(2,1)S(1)} %get-tuple-element.54), channel_id=1, source_target_pairs={{0,1},{1,2},{2,3},{3,4},{4,5},{5,6},{6,7},{8,9},{9,10},{10,11},{11... | collective-permute-start | bytes 96776 | tf_op jit(solution)/shard_map/ppermute | solution.py:19
  21.3 1.0 %slice_reduce_fusion.49 = (f32[384]{0:T(512)S(1)}, f32[384]{0:T(512)S(1)}, f32[384]{0:T(512)S(1)}, f32[384]{0:T(512)S(1)}, f32[384]{0:T(512)S(1)}, /*index=5*/f3...) fusion(f32[7,7,384]{2,1,0:T(8,128)} %param.17), kind=kLoop, calls=%fused_computation.295 | loop fusion | bytes 33792 | tf_op jit(solution)/shard_map/slice | solution.py:105
  22.3 0.1 copy.35
  22.4 0.1 broadcast_in_dim.30
  22.5 0.1 gt.20
  22.6 0.1 pad.11.clone
  22.7 0.0 collective-permute-done.3
  22.7 0.0 collective-permute-done.2
  22.7 0.0 copy-done.1
  22.7 0.0 copy-start.8
  22.7 0.0 copy-start.9
  22.7 0.0 copy-start.10
  22.7 0.0 copy-start.11
  22.8 0.0 copy-start.12
  22.8 4.2 %fusion.161 = (f32[8,32]{1,0:T(8,128)S(1)}, f32[8,32,384]{2,1,0:T(8,128)S(1)}) fusion(f32[384]{0:T(512)S(1)} %get-tuple-element.50, bf16[14,3,384]{2,1,0:T(4,128)(2,1)S(1)} %collective-permute-done.3, bf16[14,32,384]{2,1,0:T(8,128)(2,1)S(1)} %get-tuple-element.64, f32[384]{0:T(512)S(1)} %get-tuple-element.51, f32[384]{0:T(512)S(1)} %get-tuple-element.4, ...), kind=kLoop, calls=%fused_computation.338 | loop fusion | flops 26935040 | bytes 2255872 | tf_op jit(solution)/shard_map/reduce_sum | solution.py:107
  27.0 0.2 multiply_reduce_fusion
  27.2 0.1 add_convert_fusion
  27.4 0.0 copy-start.3
  27.4 5.5 %fusion.14 = bf16[256,384]{1,0:T(8,128)(2,1)S(1)} fusion(bf16[1536,384]{1,0:T(8,128)(2,1)S(1)} %copy-done, bf16[256,384]{1,0:T(8,128)(2,1)S(1)} %bitcast.44, bf16[384,1536]{1,0:T(8,128)(2,1)} %param.21, f32[1536]{0:T(1024)S(1)} %copy-done.10, f32[384]{0:T(512)S(1)} %copy-done.11, f32[384]{0:T(512)S(1)} %copy-done.12, bf16[256,384]{1,0:T(8,128)(2,1)S(1)} %bitcast.37), kind=kOutput, calls=%fused_computation.66 | convolution fusion | flops 630423552 | bytes 2958336 | tf_op jit(solution)/shard_map/dot_general | solution.py:118
  32.9 0.0 copy-start.2
  32.9 0.0 copy-start.4
  32.9 0.3 convolution_convert_fusion
  33.2 0.1 copy.30
  33.3 0.4 fusion.164
  33.7 0.3 fusion.49
  34.0 0.1 copy.34
  34.1 0.1 copy.33
  34.2 0.0 copy-done.4
  34.2 0.3 convolution_convert_fusion.1
  34.5 0.1 copy.29
  34.6 0.3 convolution_bitcast_fusion
  34.9 0.2 copy.32
  35.1 0.1 concatenate.81
  35.2 0.0 copy-start.6
  35.2 0.7 maximum_maximum_fusion
  35.9 3.8 %all-to-all-start = ((f32[8,8,512]{2,1,0:T(8,128)}), f32[8,8,512]{2,1,0:T(8,128)S(1)}, u32[]{:S(2)}, u32[]{:S(2)}) async-start(f32[8,8,512]{2,1,0:T(8,128)} %maximum_maximum_fusion), calls=%async_computation | async-start | bytes 262144 | tf_op jit(solution)/shard_map/all_to_all | solution.py:66
  39.8 5.3 %all-to-all-done = f32[8,8,512]{2,1,0:T(8,128)S(1)} async-done(((f32[8,8,512]{2,1,0:T(8,128)}), f32[8,8,512]{2,1,0:T(8,128)S(1)}, u32[]{:S(2)}, u32[]{:S(2)}) %all-to-all-start) | async-done | bytes 131104 | tf_op jit(solution)/shard_map/all_to_all | solution.py:66
  45.1 0.1 fusion.98
  45.2 0.1 fusion.15
  45.3 0.1 maximum_maximum_fusion.1
  45.4 18.4 %all_to_all.20 = f32[8,8,512]{2,1,0:T(8,128)S(1)} all-to-all(f32[8,8,512]{2,1,0:T(8,128)S(1)} %broadcast_in_dim.64), channel_id=1, replica_groups={{0,64,128,192,256,320,384,448},{8,72,136,200,264,328,392,456},{16,80,14..., dimensions={0} | all-to-all | bytes 262144 | tf_op jit(solution)/shard_map/all_to_all | solution.py:58
  63.8 0.1 fusion.97
  63.9 0.1 fusion.16
  64.0 0.1 maximum_maximum_fusion.2
  64.1 16.5 %all_to_all.21 = f32[8,8,512]{2,1,0:T(8,128)S(1)} all-to-all(f32[8,8,512]{2,1,0:T(8,128)S(1)} %broadcast_in_dim.65), channel_id=1, replica_groups=mesh['row'=64,'col'=8] {'col'}, dimensions={0} | all-to-all | bytes 262144 | tf_op jit(solution)/shard_map/all_to_all | solution.py:58
  80.7 0.1 fusion.17
  80.8 0.1 fusion.96
  80.9 0.1 convolution_multiply_fusion.4
  81.0 11.2 %all_to_all.22 = f32[8,8,384]{2,1,0:T(8,128)S(1)} all-to-all(f32[8,8,384]{2,1,0:T(8,128)S(1)} %broadcast_in_dim.66), channel_id=1, replica_groups={{0,8,16,24,32,40,48,56},{64,72,80,88,96,104,112,120},{128,136,144,152,1..., dimensions={0} | all-to-all | bytes 196608 | tf_op jit(solution)/shard_map/all_to_all | solution.py:58
  92.2 0.3 convolution_reduce_fusion
  92.5 0.6 fusion.121
  93.2 0.6 copy.41
  (30 shorter events, 0.2 us)
Async XLA Ops:
  0.6 26.8 %copy-start = (bf16[1536,384]{1,0:T(8,128)(2,1)S(1)}, bf16[1536,384]{1,0:T(8,128)(2,1)}, u32[]{:S(2)}) copy-start(bf16[1536,384]{1,0:T(8,128)(2,1)} %param.23) | copy-start | bytes 3538948
  0.6 22.1 %copy-start.1 = (bf16[8,32,384]{2,1,0:T(8,128)(2,1)S(1)}, bf16[8,32,384]{2,1,0:T(8,128)(2,1)}, u32[]{:S(2)}) copy-start(bf16[8,32,384]{2,1,0:T(8,128)(2,1)} %param.16) | copy-start | bytes 589828
  0.7 21.6 %copy-start.5 = (bf16[64,384]{1,0:T(8,128)(2,1)S(1)}, bf16[64,384]{1,0:T(8,128)(2,1)}, u32[]{:S(2)}) copy-start(bf16[64,384]{1,0:T(8,128)(2,1)} %param.28) | copy-start | bytes 147460
  0.7 22.0 %copy-start.7 = (f32[384]{0:T(512)S(1)}, f32[384]{0:T(512)}, u32[]{:S(2)}) copy-start(f32[384]{0:T(512)} %param.18) | copy-start | bytes 4612
  1.7 13.2 %collective-permute-start = (bf16[3,32,384]{2,1,0:T(8,128)(2,1)S(1)}, bf16[3,32,384]{2,1,0:T(8,128)(2,1)S(1)}, u32[]{:S(2)}, u32[]{:S(2)}) collective-permute-start(bf16[3,32,384]{2,1,0:T(8,128)(2,1)S(1)} %get-tuple-element.60), channel_id=1, source_target_pairs={{0,8},{8,16},{16,24},{24,32},{32,40},{40,48},{48,56},{56,64},{64,7... | collective-permute-start | bytes 221192 | tf_op jit(solution)/shard_map/ppermute | solution.py:19
  6.2 9.7 %collective-permute-start.1 = (bf16[3,32,384]{2,1,0:T(8,128)(2,1)S(1)}, bf16[3,32,384]{2,1,0:T(8,128)(2,1)S(1)}, u32[]{:S(2)}, u32[]{:S(2)}) collective-permute-start(bf16[3,32,384]{2,1,0:T(8,128)(2,1)S(1)} %get-tuple-element.59), channel_id=1, source_target_pairs={{8,0},{16,8},{24,16},{32,24},{40,32},{48,40},{56,48},{64,56},{72,6... | collective-permute-start | bytes 221192 | tf_op jit(solution)/shard_map/ppermute | solution.py:22
  16.0 6.7 %collective-permute-start.3 = (bf16[14,3,384]{2,1,0:T(4,128)(2,1)S(1)}, bf16[14,3,384]{2,1,0:T(4,128)(2,1)S(1)}, u32[]{:S(2)}, u32[]{:S(2)}) collective-permute-start(bf16[14,3,384]{2,1,0:T(4,128)(2,1)S(1)} %get-tuple-element.55), channel_id=1, source_target_pairs={{1,0},{2,1},{3,2},{4,3},{5,4},{6,5},{7,6},{9,8},{10,9},{11,10},{12... | collective-permute-start | bytes 96776 | tf_op jit(solution)/shard_map/ppermute | solution.py:22
  17.3 5.4 %collective-permute-start.2 = (bf16[14,3,384]{2,1,0:T(4,128)(2,1)S(1)}, bf16[14,3,384]{2,1,0:T(4,128)(2,1)S(1)}, u32[]{:S(2)}, u32[]{:S(2)}) collective-permute-start(bf16[14,3,384]{2,1,0:T(4,128)(2,1)S(1)} %get-tuple-element.54), channel_id=1, source_target_pairs={{0,1},{1,2},{2,3},{3,4},{4,5},{5,6},{6,7},{8,9},{9,10},{10,11},{11... | collective-permute-start | bytes 96776 | tf_op jit(solution)/shard_map/ppermute | solution.py:19
  22.7 4.5 %copy-start.8 = (f32[384]{0:T(512)S(1)}, f32[384]{0:T(512)}, u32[]{:S(2)}) copy-start(f32[384]{0:T(512)} %param.20) | copy-start | bytes 4612
  22.7 4.5 %copy-start.9 = (f32[384]{0:T(512)S(1)}, f32[384]{0:T(512)}, u32[]{:S(2)}) copy-start(f32[384]{0:T(512)} %param.19) | copy-start | bytes 4612
  22.7 4.7 %copy-start.10 = (f32[1536]{0:T(1024)S(1)}, f32[1536]{0:T(1024)}, u32[]{:S(2)}) copy-start(f32[1536]{0:T(1024)} %param.22) | copy-start | bytes 18436
  22.7 4.7 %copy-start.11 = (f32[384]{0:T(512)S(1)}, f32[384]{0:T(512)}, u32[]{:S(2)}) copy-start(f32[384]{0:T(512)} %param.24) | copy-start | bytes 4612
  22.8 4.7 %copy-start.12 = (f32[384]{0:T(512)S(1)}, f32[384]{0:T(512)}, u32[]{:S(2)}) copy-start(f32[384]{0:T(512)} %param.25) | copy-start | bytes 4612
  27.4 5.5 %copy-start.3 = (bf16[384,384]{1,0:T(8,128)(2,1)S(1)}, bf16[384,384]{1,0:T(8,128)(2,1)}, u32[]{:S(2)}) copy-start(bf16[384,384]{1,0:T(8,128)(2,1)} %param.26) | copy-start | bytes 884740
  32.9 1.3 %copy-start.2 = (bf16[256,384]{1,0:T(8,128)(2,1)}, bf16[256,384]{1,0:T(8,128)(2,1)S(1)}, u32[]{:S(2)}) copy-start(bf16[256,384]{1,0:T(8,128)(2,1)S(1)} %fusion.14) | copy-start | bytes 589828
  32.9 1.3 %copy-start.4 = (bf16[384,384]{1,0:T(8,128)(2,1)S(1)}, bf16[384,384]{1,0:T(8,128)(2,1)}, u32[]{:S(2)}) copy-start(bf16[384,384]{1,0:T(8,128)(2,1)} %param.27) | copy-start | bytes 884740
  35.2 57.0 %copy-start.6 = (f32[384,16]{0,1:T(8,128)S(1)}, f32[384,16]{0,1:T(8,128)}, u32[]{:S(2)}) copy-start(f32[384,16]{0,1:T(8,128)} %param.29) | copy-start | bytes 73732
  35.9 56.6 %copy-start.13 = (s32[16]{0:T(128)S(1)}, s32[16]{0:T(128)}, u32[]{:S(2)}) copy-start(s32[16]{0:T(128)} %param.31) | copy-start | bytes 196
  35.9 9.1 %all-to-all-start = ((f32[8,8,512]{2,1,0:T(8,128)}), f32[8,8,512]{2,1,0:T(8,128)S(1)}, u32[]{:S(2)}, u32[]{:S(2)}) async-start(f32[8,8,512]{2,1,0:T(8,128)} %maximum_maximum_fusion), calls=%async_computation | async-start | bytes 262144 | tf_op jit(solution)/shard_map/all_to_all | solution.py:66
where the time goes:
time: 94.5 us; the launch traced here: 93.8 us
  blocking collectives  46.1 us (49%)
  starting transfers between devices  19.2 us (20%)
  matrix products  7.52 us (8%)
  local copies, waits for them, and re-layouts  7.38 us (8%)
  other arithmetic  7.31 us (8%)
  waiting for transfers between devices  5.28 us (6%)
  between operations  1.06 us (1%)
    all_to_all x3, blocking collectives, everyone(): lax.all_to_all(jnp.broadcast_to(part[None], (8,) + part.shape), axis, 0,...  46.1 us
    ppermute x2, starting transfers between devices, with_halo(): lax.ppermute(lax.slice_in_dim(block, block.shape[dim] - width, None, axis...  8.5 us
    ppermute x2, starting transfers between devices, with_halo(): lax.ppermute(lax.slice_in_dim(block, 0, width, axis=dim), axis, backward)  6.86 us
    dot_general x1, matrix products, per_device(): jnp.dot(hidden, shrink_weight, preferred_element_type=jnp.float32)  5.46 us
    all_to_all x1, waiting for transfers between devices, merged(): lax.all_to_all(rows, 'row', 0, 0, axis_index_groups=NEAR, tiled=True)  5.27 us
    reduce_sum x1, other arithmetic, per_device(): center = jnp.mean(conv, axis=-1, keepdims=True)  4.23 us
    all_to_all x1, starting transfers between devices, merged(): lax.all_to_all(rows, 'row', 0, 0, axis_index_groups=NEAR, tiled=True)  3.83 us
    slice x3, local copies, waits for them, and re-layouts, per_device(): depth_weight[offset_row, offset_col]  3.35 us
  transfers between devices with their start and end apart: 5, of which 1 were waited for; matrix products, arithmetic and copies ran while one was open for 6% of the time, Pallas kernels for 0%

commit v1 on v0

v1 whole, which is shorter than its diff:
```python
import jax
import jax.numpy as jnp
from jax import lax
from jax.experimental import pallas as pl
from jax.experimental.pallas import tpu as pltpu
from jax.sharding import PartitionSpec as P

NH = 8
NQ = 64
TILE = 8
LOG2E = 1.4426950408889634
NEAR = [[z * 8 + r for r in range(8)] for z in range(8)]
FAR = [[z * 8 + r for z in range(8)] for r in range(8)]


WIDTH = 384
LANES = 128
CELLS_R = 8
CELLS_C = 32
HID = 1536


def taps(acc, rows, weight_ref, lanes, b, first):
    for a in range(7):
        weight = weight_ref[a, b : b + 1, lanes]
        for i in range(CELLS_R):
            at = i + a - 3 - first
            if 0 <= at < len(rows):
                acc[i] = acc[i] + rows[at] * weight
    return acc


def own_kernel(
    x_hbm,
    weight_hbm,
    expand_hbm,
    shrink_hbm,
    key_hbm,
    value_hbm,
    query_hbm,
    bias_hbm,
    gain_hbm,
    norm_bias_hbm,
    shrink_bias_hbm,
    scale_hbm,
    expand_bias_hbm,
    acc_ref,
    first_ref,
    last_ref,
    x_ref,
    weight_ref,
    expand_ref,
    shrink_ref,
    key_ref,
    turned_ref,
    big_ref,
    rows_ref,
    wide,
    value_ref,
    query_ref,
    bias_ref,
    gain_ref,
    norm_bias_ref,
    shrink_bias_ref,
    scale_ref,
    expand_bias_ref,
    sems,
):
    pairs = (
        (x_hbm, x_ref),
        (weight_hbm, weight_ref),
        (bias_hbm, bias_ref),
        (query_hbm, query_ref),
        (value_hbm, value_ref),
        (gain_hbm, gain_ref),
        (norm_bias_hbm, norm_bias_ref),
        (shrink_bias_hbm, shrink_bias_ref),
        (scale_hbm, scale_ref),
        (expand_bias_hbm, expand_bias_ref),
        (key_hbm, key_ref),
        (expand_hbm, expand_ref),
        (shrink_hbm, shrink_ref),
    )
    copies = [pltpu.make_async_copy(s, d, sems.at[k]) for k, (s, d) in enumerate(pairs)]
    for copy in copies:
        copy.start()
    for copy in copies[:3]:
        copy.wait()
    rows_ref[8:9, :] = bias_ref[...].reshape(1, WIDTH)
    first_ref[...] = x_ref[:, 0:3, :]
    last_ref[...] = x_ref[:, CELLS_C - 3 : CELLS_C, :]
    for c in range(3):
        lanes = pl.ds(c * LANES, LANES)
        wide[c, :, 0:8, :] = jnp.zeros((CELLS_R, 8, LANES), jnp.float32)
        wide[c, :, 8 + CELLS_C : 16 + CELLS_C, :] = jnp.zeros((CELLS_R, 8, LANES), jnp.float32)
        wide[c, :, 8 : 8 + CELLS_C, :] = x_ref[:, :, lanes].astype(jnp.float32)

    def lane_tile(c, carry):
        lanes = pl.ds(pl.multiple_of(c * LANES, LANES), LANES)
        bias = jnp.broadcast_to(rows_ref[8:9, lanes], (8, LANES))
        for j in range(CELLS_C // 8):
            acc = [bias] * CELLS_R
            for b in range(7):
                at = 8 * j + 5 + b
                rows = [wide[c, r, at : at + 8, :] for r in range(CELLS_R)]
                acc = taps(acc, rows, weight_ref, lanes, b, 0)
            for i in range(CELLS_R):
                acc_ref[i, 8 * j : 8 * j + 8, lanes] = acc[i]
        return carry

    lax.fori_loop(0, 3, lane_tile, 0)
    for copy in copies[3:]:
        copy.wait()
    for row, ref in enumerate((gain_ref, norm_bias_ref, shrink_bias_ref, scale_ref)):
        rows_ref[row : row + 1, :] = ref[...].reshape(1, WIDTH)
    for k in range(HID // WIDTH):
        rows_ref[4 + k : 5 + k, :] = expand_bias_ref[k * WIDTH : (k + 1) * WIDTH].reshape(1, WIDTH)
    turned_ref[...] = value_ref[...].astype(jnp.float32).T.astype(jnp.bfloat16)
    query = query_ref[...].astype(jnp.float32)
    query = jnp.concatenate([query, query], axis=0).T
    head = lax.broadcasted_iota(jnp.int32, (WIDTH, LANES), 0) // (WIDTH // NH)
    half = lax.broadcasted_iota(jnp.int32, (WIDTH, LANES), 1) // NQ
    for t in range(NH // 2):
        big_ref[:, t * LANES : (t + 1) * LANES] = jnp.where(
            head == 2 * t + half, query, 0.0
        ).astype(jnp.bfloat16)


def rows_kernel(acc_in, low_ref, high_ref, weight_ref, acc_ref, wide):
    for c in range(3):
        lanes = pl.ds(c * LANES, LANES)
        wide[c, :, 0:8, :] = jnp.zeros((6, 8, LANES), jnp.float32)
        wide[c, :, 8 + CELLS_C : 16 + CELLS_C, :] = jnp.zeros((6, 8, LANES), jnp.float32)
        wide[c, 0:3, 8 : 8 + CELLS_C, :] = low_ref[:, :, lanes].astype(jnp.float32)
        wide[c, 3:6, 8 : 8 + CELLS_C, :] = high_ref[:, :, lanes].astype(jnp.float32)

    def lane_tile(c, carry):
        lanes = pl.ds(pl.multiple_of(c * LANES, LANES), LANES)
        for j in range(CELLS_C // 8):
            acc = [acc_in[i, 8 * j : 8 * j + 8, lanes] for i in range(CELLS_R)]
            for b in range(7):
                at = 8 * j + 5 + b
                rows = [wide[c, r, at : at + 8, :] for r in range(6)]
                acc = taps(acc, rows[:3], weight_ref, lanes, b, -3)
                acc = taps(acc, rows[3:], weight_ref, lanes, b, CELLS_R)
            for i in range(CELLS_R):
                acc_ref[i, 8 * j : 8 * j + 8, lanes] = acc[i]
        return carry

    lax.fori_loop(0, 3, lane_tile, 0)


def gelu(x):
    return 0.5 * x * (1.0 + lax.erf(x * (0.5**0.5)))


def marked(weighted, marks):
    high = marks.astype(jnp.bfloat16).astype(jnp.float32)
    rest = marks - high
    middle = rest.astype(jnp.bfloat16).astype(jnp.float32)
    low = (rest - middle).astype(jnp.bfloat16).astype(jnp.float32)
    marks = high + pltpu.roll(middle, NH, 1) + pltpu.roll(low, 2 * NH, 1)
    return jnp.concatenate([weighted, marks], axis=1).astype(jnp.bfloat16)


def cells_kernel(
    tissue_ref,
    acc_ref,
    left_ref,
    right_ref,
    weight_ref,
    x_ref,
    rows_ref,
    expand_ref,
    shrink_ref,
    key_ref,
    turned_ref,
    big_ref,
    out_ref,
    part_ref,
    edge,
    normed,
    hidden,
    sums,
):
    count = CELLS_R * CELLS_C
    tall = CELLS_R + 6
    edge[...] = jnp.zeros(edge.shape, jnp.float32)
    for c in range(3):
        lanes = pl.ds(c * LANES, LANES)
        edge[0, c, :, 5:8, :] = left_ref[:, :, lanes].astype(jnp.float32)
        edge[1, c, :, 8:11, :] = right_ref[:, :, lanes].astype(jnp.float32)

    def lane_tile(c, carry):
        lanes = pl.ds(pl.multiple_of(c * LANES, LANES), LANES)
        for side, j in ((0, 0), (1, CELLS_C // 8 - 1)):
            acc = [acc_ref[i, 8 * j : 8 * j + 8, lanes] for i in range(CELLS_R)]
            for b in (0, 1, 2) if side == 0 else (4, 5, 6):
                at = 5 + b if side == 0 else b - 3
                rows = [edge[side, c, r, at : at + 8, :] for r in range(tall)]
                acc = taps(acc, rows, weight_ref, lanes, b, -3)
            for i in range(CELLS_R):
                acc_ref[i, 8 * j : 8 * j + 8, lanes] = acc[i]
        return carry

    lax.fori_loop(0, 3, lane_tile, 0)
    gain, norm_bias, shrink_bias, scale = (rows_ref[k : k + 1, :] for k in range(4))
    for i in range(CELLS_R):
        conv = acc_ref[i]
        center = jnp.mean(conv, axis=-1, keepdims=True)
        conv = conv - center
        variance = jnp.mean(conv * conv, axis=-1, keepdims=True)
        normed[i * CELLS_C : (i + 1) * CELLS_C, :] = (
            conv * lax.rsqrt(variance + 1e-06) * gain + norm_bias
        ).astype(jnp.bfloat16)
    for k in range(HID // WIDTH):
        lanes = slice(k * WIDTH, (k + 1) * WIDTH)
        part = jnp.dot(normed[...], expand_ref[:, lanes], preferred_element_type=jnp.float32)
        hidden[:, lanes] = gelu(part + rows_ref[4 + k : 5 + k, :]).astype(jnp.bfloat16)
    shrunk = jnp.dot(hidden[...], shrink_ref[...], preferred_element_type=jnp.float32)
    shrunk = shrunk + shrink_bias
    block = (x_ref[...].reshape(count, WIDTH).astype(jnp.float32) + scale * shrunk).astype(
        jnp.bfloat16
    )
    out_ref[...] = block.reshape(CELLS_R, CELLS_C, WIDTH)
    keys = jnp.dot(block, key_ref[...], preferred_element_type=jnp.float32).astype(jnp.bfloat16)
    values = lax.dot_general(
        turned_ref[...], block, (((1,), (1,)), ((), ())), preferred_element_type=jnp.float32
    ).astype(jnp.bfloat16)
    size = WIDTH // NH
    groups = CELLS_C // TILE
    line = lax.broadcasted_iota(jnp.int32, (NH, LANES), 0)
    tops = jnp.zeros((NH, LANES), jnp.float32)
    totals = jnp.zeros((NH, LANES), jnp.float32)
    for t in range(NH // 2):
        scores = jnp.dot(
            keys, big_ref[:, t * LANES : (t + 1) * LANES], preferred_element_type=jnp.float32
        ) * (size**-0.5 * LOG2E)
        scores = scores.reshape(CELLS_R, groups, TILE, LANES)
        scores = [jnp.where(tissue_ref[0, g] > 0, scores[:, g], -1e30) for g in range(groups)]
        top = scores[0]
        for g in range(1, groups):
            top = jnp.maximum(top, scores[g])
        top = jnp.ceil(jnp.max(jnp.max(top, axis=0), axis=0, keepdims=True))
        weights = [
            jnp.where(tissue_ref[0, g] > 0, jnp.exp2(scores[g] - top), 0.0) for g in range(groups)
        ]
        total = weights[0]
        for g in range(1, groups):
            total = total + weights[g]
        total = jnp.sum(jnp.sum(total, axis=0), axis=0, keepdims=True)
        weights = jnp.stack(weights, axis=1).reshape(count, LANES).astype(jnp.bfloat16)
        pair = jnp.dot(
            values[2 * size * t : 2 * size * (t + 1), :], weights, preferred_element_type=jnp.float32
        )
        sums[2 * size * t : 2 * size * t + size, :] = pair[:size]
        sums[2 * size * t + size : 2 * size * (t + 1), :] = pltpu.roll(pair[size:], NQ, 1)
        tops = jnp.where(line == 2 * t, top, tops)
        tops = jnp.where(line == 2 * t + 1, pltpu.roll(jnp.broadcast_to(top, (NH, LANES)), NQ, 1), tops)
        totals = jnp.where(line == 2 * t, total, totals)
        totals = jnp.where(
            line == 2 * t + 1, pltpu.roll(jnp.broadcast_to(total, (NH, LANES)), NQ, 1), totals
        )
    sums[WIDTH:, :] = jnp.zeros((LANES, LANES), jnp.float32)
    sums[WIDTH : WIDTH + NH, :] = tops
    sums[WIDTH + 3 * NH : WIDTH + 4 * NH, :] = totals
    part = sums[...].T
    part_ref[...] = marked(part[:NQ, :WIDTH], part[:NQ, WIDTH:])


def spread_matrix(first, copies):
    lane = lax.broadcasted_iota(jnp.int32, (LANES, WIDTH), 0) - first
    head = lax.broadcasted_iota(jnp.int32, (LANES, WIDTH), 1) // (WIDTH // NH)
    inside = (lane >= 0) & (lane < copies * NH)
    return jnp.where(inside & (lane % NH == head), 1.0, 0.0).astype(jnp.bfloat16)


def combined(parts):
    n, q = parts.shape[:2]
    parts = parts.astype(jnp.float32)
    marks = parts[:, :, WIDTH:].reshape(n * q, LANES)
    marks = marks + pltpu.roll(marks, LANES - NH, 1) + pltpu.roll(marks, LANES - 2 * NH, 1)
    top = jnp.max(marks.reshape(n, q, LANES), axis=0)
    factor = jnp.exp2(marks.reshape(n, q, LANES) - top).reshape(n * q, LANES)
    factor = factor.astype(jnp.bfloat16)
    spread = jnp.dot(factor, spread_matrix(0, 1), preferred_element_type=jnp.float32)
    weighted = jnp.sum(parts[:, :, :WIDTH] * spread.reshape(n, q, WIDTH), axis=0)
    total = marks * pltpu.roll(factor.astype(jnp.float32), 3 * NH, 1)
    total = jnp.sum(total.reshape(n, q, LANES), axis=0)
    lane = lax.broadcasted_iota(jnp.int32, (q, LANES), 1)
    inside = (lane >= 3 * NH) & (lane < 4 * NH)
    return weighted, jnp.where(lane < NH, top, 0.0), jnp.where(inside, total, 1.0), inside


def merge_kernel(parts_ref, out_ref):
    weighted, top, total, inside = combined(parts_ref[...])
    part = marked(weighted, top + jnp.where(inside, total, 0.0))
    out_ref[...] = jnp.broadcast_to(part[None], out_ref.shape)


def pool_kernel(parts_ref, out_ref):
    weighted, _, total, inside = combined(parts_ref[...])
    marks = marked(weighted, jnp.where(inside, 1.0 / total, 0.0))[:, WIDTH:]
    inverse = jnp.dot(marks, spread_matrix(3 * NH, 3), preferred_element_type=jnp.float32)
    out_ref[...] = jnp.broadcast_to((weighted * inverse)[None], out_ref.shape)


def loss_kernel(pooled_ref, class_ref, label_ref, out_ref, loss_ref):
    pooled = pooled_ref[...]
    out_ref[...] = pooled
    lines = jnp.sum(pooled.reshape(NQ // 8, 8, WIDTH), axis=0)
    logits = jnp.dot(
        lines, class_ref[...], precision=lax.Precision.HIGHEST, preferred_element_type=jnp.float32
    )
    logits = jnp.sum(logits, axis=0, keepdims=True)
    label = label_ref[...].reshape(logits.shape).astype(jnp.float32)
    soft = jnp.maximum(logits, 0.0) + jnp.log1p(jnp.exp(-jnp.abs(logits)))
    loss_ref[0] = jnp.sum(soft - label * logits)


def everyone(part, axis, groups=None):
    return lax.all_to_all(part, axis, 0, 0, axis_index_groups=groups, tiled=True)


def call(kernel, out_shape, name, *args, **more):
    return pl.pallas_call(kernel, out_shape=out_shape, name=name, **more, **params())(*args)


def merged(part, class_weight, slide_label):
    chunk = (8, NQ // 8, WIDTH + LANES)
    same = jax.ShapeDtypeStruct(chunk, jnp.bfloat16)
    parts = everyone(part.reshape(chunk), "row", NEAR)
    parts = everyone(call(merge_kernel, same, "merge_near", parts), "row", FAR)
    parts = everyone(call(merge_kernel, same, "merge_far", parts), "col")
    rows = jax.ShapeDtypeStruct((8, NQ // 8, WIDTH), jnp.float32)
    pooled = everyone(call(pool_kernel, rows, "pool", parts), "row", NEAR)
    return call(
        loss_kernel,
        (jax.ShapeDtypeStruct((NQ, WIDTH), jnp.float32), jax.ShapeDtypeStruct((1,), jnp.float32)),
        "loss",
        pooled.reshape(NQ, WIDTH),
        class_weight,
        slide_label,
        out_specs=(pl.BlockSpec(memory_space=pltpu.VMEM), pl.BlockSpec(memory_space=pltpu.SMEM)),
    )


def vmem(*shape):
    return pltpu.VMEM(shape, jnp.float32)


def params(flops=1000000):
    return dict(
        compiler_params=pltpu.CompilerParams(vmem_limit_bytes=24 * 1024 * 1024),
        cost_estimate=pl.CostEstimate(flops=flops, bytes_accessed=1000000, transcendentals=0),
    )


def exchanged(first, last, axis):
    count = lax.axis_size(axis)
    forward = [(i, i + 1) for i in range(count - 1)]
    backward = [(target, source) for source, target in forward]
    return lax.ppermute(last, axis, forward), lax.ppermute(first, axis, backward)


def per_device(
    features,
    depth_weight,
    depth_bias,
    norm_gain,
    norm_bias,
    expand_weight,
    expand_bias,
    shrink_weight,
    shrink_bias,
    layer_scale,
    key_weight,
    value_weight,
    queries,
    class_weight,
    tissue,
    slide_label,
):
    rows, cols, width = features.shape
    f32, bf16 = jnp.float32, jnp.bfloat16
    hbm, whole = pl.BlockSpec(memory_space=pltpu.HBM), pl.BlockSpec(memory_space=pltpu.VMEM)
    shaped = jax.ShapeDtypeStruct
    low, high = exchanged(features[:3], features[-3:], "row")
    acc, first, last, cells, taps_, expand, shrink, key, turned, big, lines = call(
        own_kernel,
        (
            shaped((rows, cols, width), f32),
            shaped((rows, 3, width), bf16),
            shaped((rows, 3, width), bf16),
            shaped(features.shape, bf16),
            shaped(depth_weight.shape, f32),
            shaped(expand_weight.shape, bf16),
            shaped(shrink_weight.shape, bf16),
            shaped(key_weight.shape, bf16),
            shaped(value_weight.shape, bf16),
            shaped((width, NH * NQ), bf16),
            shaped((16, width), f32),
        ),
        "own_cells",
        *(
            pltpu.with_memory_space_constraint(array, pltpu.HBM)
            for array in (
                features,
                depth_weight,
                expand_weight,
                shrink_weight,
                key_weight,
                value_weight,
                queries,
                depth_bias,
                norm_gain,
                norm_bias,
                shrink_bias,
                layer_scale,
                expand_bias,
            )
        ),
        in_specs=[hbm] * 13,
        out_specs=(whole,) * 11,
        scratch_shapes=[
            vmem(3, rows, cols + 16, LANES),
            pltpu.VMEM(value_weight.shape, bf16),
            pltpu.VMEM(queries.shape, bf16),
            *(vmem(width) for _ in range(5)),
            vmem(HID),
            pltpu.SemaphoreType.DMA((13,)),
        ],
    )
    left, right = exchanged(
        jnp.concatenate([low[:, :3], first, high[:, :3]], axis=0),
        jnp.concatenate([low[:, -3:], last, high[:, -3:]], axis=0),
        "col",
    )
    acc = call(
        rows_kernel,
        shaped((rows, cols, width), f32),
        "halo_rows",
        acc,
        low,
        high,
        taps_,
        scratch_shapes=[vmem(3, 6, cols + 16, LANES)],
        input_output_aliases={0: 0},
    )
    block_out, part = call(
        cells_kernel,
        (shaped((rows, cols, width), bf16), shaped((NQ, width + LANES), bf16)),
        "cells",
        tissue,
        acc,
        left,
        right,
        taps_,
        cells,
        lines,
        expand,
        shrink,
        key,
        turned,
        big,
        in_specs=[pl.BlockSpec(memory_space=pltpu.SMEM)] + [whole] * 11,
        scratch_shapes=[
            vmem(2, 3, rows + 6, 16, LANES),
            pltpu.VMEM((rows * cols, width), bf16),
            pltpu.VMEM((rows * cols, HID), bf16),
            vmem(width + LANES, LANES),
        ],
    )
    pooled, slide_loss = merged(part, class_weight, slide_label)
    return (block_out, pooled, slide_loss)


def solution(mesh):
    placed = (P("row", "col", None),) + (P(),) * 13 + (P("row", "col"), P())
    return jax.shard_map(
        per_device,
        mesh=mesh,
        in_specs=placed,
        out_specs=(P("row", "col", None), P(), P()),
        check_vma=False,
    )
```

time: 94.5 us -> 80.9 us (0.86)
  Pallas kernels: 0 us -> 9.11 us
  matrix products: 7.52 us -> 0 us
  other arithmetic: 7.31 us -> 0.08 us
  local copies, waits for them, and re-layouts: 7.38 us -> 1.1 us
  blocking collectives: 46.1 us -> 41.5 us
  waiting for transfers between devices: 5.28 us -> 8.36 us
    pallas_call x0 -> x7, Pallas kernels: none -> 9.11 us  [call(): pl.pallas_call(kernel, out_shape=out_shape, name=name, **more, **params())]
    dot_general x10 -> x0, matrix products: 7.52 us -> none  [the longest x1 5.46 us: per_device(): jnp.dot(hidden, shrink_weight, preferred_element_type=jnp.float32)]
    reduce_sum x7 -> x0, other arithmetic: 5.55 us -> none  [the longest x1 4.23 us: per_device(): center = jnp.mean(conv, axis=-1, keepdims=True)]
    all_to_all x3, blocking collectives: 46.1 us -> 41.5 us  [everyone(): lax.all_to_all(part, axis, 0, 0, axis_index_groups=groups, tiled=True)]
    ppermute x4, waiting for transfers between devices: 0.01 us -> 3.49 us  [the longest x2 3.48 us: exchanged(): lax.ppermute(first, axis, backward)]
    slice x5 -> x3, local copies, waits for them, and re-layouts: 4.44 us -> 0.96 us  [the longest x1 0.94 us: per_device(): low, high = exchanged(features[:3], features[-3:], 'row')]
    all_to_all x1, starting transfers between devices: 3.83 us -> 6.89 us  [everyone(): lax.all_to_all(part, axis, 0, 0, axis_index_groups=groups, tiled=True)]
    ppermute x4, starting transfers between devices: 15.4 us -> 12.7 us  [the longest x2 6.86 us: exchanged(): lax.ppermute(first, axis, backward)]
  transfers between devices with their start and end apart: 5 -> 5, of which waited for: 1 -> 2; matrix products, arithmetic and copies ran while one was open for 6% -> 0% of each run, Pallas kernels for 0% -> 4%
where the time goes in v1:
time: 80.9 us; the launch traced here: 80.5 us
  blocking collectives  41.5 us (51%)
  starting transfers between devices  19.6 us (24%)
  Pallas kernels  9.11 us (11%)
  waiting for transfers between devices  8.36 us (10%)
  local copies, waits for them, and re-layouts  1.1 us (1%)
    all_to_all x3, blocking collectives, everyone(): lax.all_to_all(part, axis, 0, 0, axis_index_groups=groups, tiled=True)  41.5 us
    pallas_call x7, Pallas kernels, call(): pl.pallas_call(kernel, out_shape=out_shape, name=name, **more, **params())  9.11 us
    all_to_all x1, starting transfers between devices, everyone(): lax.all_to_all(part, axis, 0, 0, axis_index_groups=groups, tiled=True)  6.89 us
    ppermute x2, starting transfers between devices, exchanged(): lax.ppermute(first, axis, backward)  6.86 us
    ppermute x2, starting transfers between devices, exchanged(): lax.ppermute(last, axis, forward)  5.8 us
    all_to_all x1, waiting for transfers between devices, everyone(): lax.all_to_all(part, axis, 0, 0, axis_index_groups=groups, tiled=True)  4.87 us
    ppermute x2, waiting for transfers between devices, exchanged(): lax.ppermute(first, axis, backward)  3.48 us
  transfers between devices with their start and end apart: 5, of which 2 were waited for; matrix products, arithmetic and copies ran while one was open for 0% of the time, Pallas kernels for 4%

profile of v1, /device:TPU:1, one launch (start us, length us, event | category | flops | bytes accessed | tf_op | source)
XLA Modules:
  0.0 80.5 jit_solution(8486381856605126732)
XLA Ops:
  0.6 0.9 %fusion = (bf16[3,32,384]{2,1,0:T(8,128)(2,1)S(1)}, bf16[3,32,384]{2,1,0:T(8,128)(2,1)S(1)}) fusion(bf16[8,32,384]{2,1,0:T(8,128)(2,1)} %x_hbm.1), kind=kLoop, calls=%fused_computation.2 | loop fusion | bytes 294912 | tf_op jit(solution)/shard_map/slice | solution.py:388
  1.6 4.5 %collective-permute-start = (bf16[3,32,384]{2,1,0:T(8,128)(2,1)S(1)}, bf16[3,32,384]{2,1,0:T(8,128)(2,1)S(1)}, u32[]{:S(2)}, u32[]{:S(2)}) collective-permute-start(bf16[3,32,384]{2,1,0:T(8,128)(2,1)S(1)} %get-tuple-element.34), channel_id=1, source_target_pairs={{0,8},{8,16},{16,24},{24,32},{32,40},{40,48},{48,56},{56,64},{64,7... | collective-permute-start | bytes 221192 | tf_op jit(solution)/shard_map/ppermute | solution.py:363
  6.1 5.6 %collective-permute-start.1 = (bf16[3,32,384]{2,1,0:T(8,128)(2,1)S(1)}, bf16[3,32,384]{2,1,0:T(8,128)(2,1)S(1)}, u32[]{:S(2)}, u32[]{:S(2)}) collective-permute-start(bf16[3,32,384]{2,1,0:T(8,128)(2,1)S(1)} %get-tuple-element.33), channel_id=1, source_target_pairs={{8,0},{16,8},{24,16},{32,24},{40,32},{48,40},{56,48},{64,56},{72,6... | collective-permute-start | bytes 221192 | tf_op jit(solution)/shard_map/ppermute | solution.py:363
  11.7 2.6 %own_cells.1 = (f32[8,32,384]{2,1,0:T(8,128)S(1)}, bf16[8,3,384]{2,1,0:T(4,128)(2,1)S(1)}, bf16[8,3,384]{2,1,0:T(4,128)(2,1)S(1)}, bf16[8,32,384]{2,1,0:T(8,128)...) custom-call(bf16[8,32,384]{2,1,0:T(8,128)(2,1)} %x_hbm.1, ...), custom_call_target="tpu_custom_call" | custom-call | flops 1000000 | bytes 1000000 | tf_op jit(solution)/shard_map/own_cells/pallas_call | solution.py:326
  14.3 0.0 copy-start
  14.3 0.0 collective-permute-done.low_ref
  14.3 0.0 collective-permute-done.1.high_ref
  14.4 1.3 %collective-permute-start.2 = (bf16[14,3,384]{2,1,0:T(4,128)(2,1)S(1)}, bf16[14,3,384]{2,1,0:T(4,128)(2,1)S(1)}, u32[]{:S(2)}, u32[]{:S(2)}) collective-permute-start(bf16[14,3,384]{2,1,0:T(4,128)(2,1)S(1)} %pad_maximum_fusion), channel_id=1, source_target_pairs={{0,1},{1,2},{2,3},{3,4},{4,5},{5,6},{6,7},{8,9},{9,10},{10,11},{11... | collective-permute-start | bytes 96776 | tf_op jit(solution)/shard_map/ppermute | solution.py:363
  15.7 1.3 %collective-permute-start.3 = (bf16[14,3,384]{2,1,0:T(4,128)(2,1)S(1)}, bf16[14,3,384]{2,1,0:T(4,128)(2,1)S(1)}, u32[]{:S(2)}, u32[]{:S(2)}) collective-permute-start(bf16[14,3,384]{2,1,0:T(4,128)(2,1)S(1)} %pad_maximum_fusion.1), channel_id=1, source_target_pairs={{1,0},{2,1},{3,2},{4,3},{5,4},{6,5},{7,6},{9,8},{10,9},{11,10},{12... | collective-permute-start | bytes 96776 | tf_op jit(solution)/shard_map/ppermute | solution.py:363
  17.0 0.4 halo_rows.1.acc_ref
  17.5 0.0 collective-permute-done.2.left_ref
  17.5 3.5 %collective-permute-done.3.right_ref = bf16[14,3,384]{2,1,0:T(4,128)(2,1)S(1)} collective-permute-done((bf16[14,3,384]{2,1,0:T(4,128)(2,1)S(1)}, bf16[14,3,384]{2,1,0:T(4,128)(2,1)S(1)}, u32[]{:S(2)}, u32[]{:S(2)}) %collective-permute-start.3) | collective-permute-done | bytes 32288 | tf_op jit(solution)/shard_map/ppermute | solution.py:363
  21.0 0.0 copy-done
  21.0 0.0 copy-start.2
  21.0 3.7 %cells.1 = (bf16[8,32,384]{2,1,0:T(8,128)(2,1)}, bf16[64,512]{1,0:T(8,128)(2,1)S(1)}) custom-call(s32[1,4]{1,0:T(1,128)S(1)} %copy-done, f32[8,32,384]{2,1,0:T(8,128)S(1)} %halo_rows.1.acc_ref, bf16[14,3,384]{2,1,0:T(4,128)(2,1)S(1)} %collective-permute-done.2.left_ref, bf16[14,3,384]{2,1,0:T(4,128)(2,1)S(1)} %collective-permute-done.3.right_ref, ...), custom_call_target="tpu_custom_call" | custom-call | flops 1000000 | bytes 1000000 | tf_op jit(solution)/shard_map/cells/pallas_call | solution.py:326
  24.6 0.0 copy-start.1
  24.7 10.6 %all_to_all.20.parts_ref = bf16[8,8,512]{2,1,0:T(8,128)(2,1)S(1)} all-to-all(bf16[8,8,512]{2,1,0:T(8,128)(2,1)S(1)} %bitcast.3), channel_id=1, replica_groups={{0,8,16,24,32,40,48,56},{64,72,80,88,96,104,112,120},{128,136,144,152,1..., dimensions={0} | all-to-all | bytes 131072 | tf_op jit(solution)/shard_map/all_to_all | solution.py:322
  35.2 0.2 merge_near.1
  35.5 16.9 %all_to_all.21.parts_ref = bf16[8,8,512]{2,1,0:T(8,128)(2,1)S(1)} all-to-all(bf16[8,8,512]{2,1,0:T(8,128)(2,1)S(1)} %merge_near.1), channel_id=1, replica_groups={{0,64,128,192,256,320,384,448},{8,72,136,200,264,328,392,456},{16,80,14..., dimensions={0} | all-to-all | bytes 131072 | tf_op jit(solution)/shard_map/all_to_all | solution.py:322
  52.3 0.2 merge_far.1
  52.6 14.1 %all_to_all.22.parts_ref = bf16[8,8,512]{2,1,0:T(8,128)(2,1)S(1)} all-to-all(bf16[8,8,512]{2,1,0:T(8,128)(2,1)S(1)} %merge_far.1), channel_id=1, replica_groups=mesh['row'=64,'col'=8] {'col'}, dimensions={0} | all-to-all | bytes 131072 | tf_op jit(solution)/shard_map/all_to_all | solution.py:322
  66.6 1.0 %pool.1 = f32[8,8,384]{2,1,0:T(8,128)} custom-call(bf16[8,8,512]{2,1,0:T(8,128)(2,1)S(1)} %all_to_all.22.parts_ref), custom_call_target="tpu_custom_call" | custom-call | flops 1000000 | bytes 1000000 | tf_op jit(solution)/shard_map/pool/pallas_call | solution.py:326
  67.7 6.9 %all-to-all-start.3 = ((f32[8,8,384]{2,1,0:T(8,128)}), f32[8,8,384]{2,1,0:T(8,128)S(1)}, u32[]{:S(2)}, u32[]{:S(2)}) async-start(f32[8,8,384]{2,1,0:T(8,128)} %pool.1), calls=%async_computation.3 | async-start | bytes 196608 | tf_op jit(solution)/shard_map/all_to_all | solution.py:322
  74.6 0.0 copy-done.2
  74.6 0.1 copy.20.class_ref
  74.7 4.9 %all-to-all-done.3 = f32[8,8,384]{2,1,0:T(8,128)S(1)} async-done(((f32[8,8,384]{2,1,0:T(8,128)}), f32[8,8,384]{2,1,0:T(8,128)S(1)}, u32[]{:S(2)}, u32[]{:S(2)}) %all-to-all-start.3) | async-done | bytes 98336 | tf_op jit(solution)/shard_map/all_to_all | solution.py:322
  79.6 0.0 copy-done.1
  79.6 0.9 %loss.1 = (f32[64,384]{1,0:T(8,128)}, f32[1]{0:T(128)}) custom-call(f32[64,384]{1,0:T(8,128)S(1)} %bitcast.2, f32[384,16]{1,0:T(8,128)S(1)} %copy.20.class_ref, s32[16]{0:T(128)S(1)} %copy-done.1), custom_call_target="tpu_custom_call" | custom-call | flops 1000000 | bytes 1000000 | tf_op jit(solution)/shard_map/loss/pallas_call | solution.py:326
  (4 shorter events, 0.1 us)
Async XLA Ops:
  1.6 12.7 %collective-permute-start = (bf16[3,32,384]{2,1,0:T(8,128)(2,1)S(1)}, bf16[3,32,384]{2,1,0:T(8,128)(2,1)S(1)}, u32[]{:S(2)}, u32[]{:S(2)}) collective-permute-start(bf16[3,32,384]{2,1,0:T(8,128)(2,1)S(1)} %get-tuple-element.34), channel_id=1, source_target_pairs={{0,8},{8,16},{16,24},{24,32},{32,40},{40,48},{48,56},{56,64},{64,7... | collective-permute-start | bytes 221192 | tf_op jit(solution)/shard_map/ppermute | solution.py:363
  6.1 8.2 %collective-permute-start.1 = (bf16[3,32,384]{2,1,0:T(8,128)(2,1)S(1)}, bf16[3,32,384]{2,1,0:T(8,128)(2,1)S(1)}, u32[]{:S(2)}, u32[]{:S(2)}) collective-permute-start(bf16[3,32,384]{2,1,0:T(8,128)(2,1)S(1)} %get-tuple-element.33), channel_id=1, source_target_pairs={{8,0},{16,8},{24,16},{32,24},{40,32},{48,40},{56,48},{64,56},{72,6... | collective-permute-start | bytes 221192 | tf_op jit(solution)/shard_map/ppermute | solution.py:363
  14.3 6.7 %copy-start = (s32[1,4]{1,0:T(1,128)S(1)}, s32[1,4]{1,0:T(1,128)}, u32[]{:S(2)}) copy-start(s32[1,4]{1,0:T(1,128)} %tissue_ref.1) | copy-start | bytes 52
  14.4 3.1 %collective-permute-start.2 = (bf16[14,3,384]{2,1,0:T(4,128)(2,1)S(1)}, bf16[14,3,384]{2,1,0:T(4,128)(2,1)S(1)}, u32[]{:S(2)}, u32[]{:S(2)}) collective-permute-start(bf16[14,3,384]{2,1,0:T(4,128)(2,1)S(1)} %pad_maximum_fusion), channel_id=1, source_target_pairs={{0,1},{1,2},{2,3},{3,4},{4,5},{5,6},{6,7},{8,9},{9,10},{10,11},{11... | collective-permute-start | bytes 96776 | tf_op jit(solution)/shard_map/ppermute | solution.py:363
  15.7 5.2 %collective-permute-start.3 = (bf16[14,3,384]{2,1,0:T(4,128)(2,1)S(1)}, bf16[14,3,384]{2,1,0:T(4,128)(2,1)S(1)}, u32[]{:S(2)}, u32[]{:S(2)}) collective-permute-start(bf16[14,3,384]{2,1,0:T(4,128)(2,1)S(1)} %pad_maximum_fusion.1), channel_id=1, source_target_pairs={{1,0},{2,1},{3,2},{4,3},{5,4},{6,5},{7,6},{9,8},{10,9},{11,10},{12... | collective-permute-start | bytes 96776 | tf_op jit(solution)/shard_map/ppermute | solution.py:363
  21.0 53.6 %copy-start.2 = (f32[384,16]{0,1:T(8,128)S(1)}, f32[384,16]{0,1:T(8,128)}, u32[]{:S(2)}) copy-start(f32[384,16]{0,1:T(8,128)} %param.29) | copy-start | bytes 73732
  24.6 54.9 %copy-start.1 = (s32[16]{0:T(128)S(1)}, s32[16]{0:T(128)}, u32[]{:S(2)}) copy-start(s32[16]{0:T(128)} %label_ref.1) | copy-start | bytes 196
  67.7 11.9 %all-to-all-start.3 = ((f32[8,8,384]{2,1,0:T(8,128)}), f32[8,8,384]{2,1,0:T(8,128)S(1)}, u32[]{:S(2)}, u32[]{:S(2)}) async-start(f32[8,8,384]{2,1,0:T(8,128)} %pool.1), calls=%async_computation.3 | async-start | bytes 196608 | tf_op jit(solution)/shard_map/all_to_all | solution.py:322

commit v2 on v1

--- a/solution.py
+++ b/solution.py
@@ -9,8 +9,21 @@
 NQ = 64
 TILE = 8
 LOG2E = 1.4426950408889634
-NEAR = [[z * 8 + r for r in range(8)] for z in range(8)]
-FAR = [[z * 8 + r for z in range(8)] for r in range(8)]
+
+
+def device(z, near, y):
+    return (z * 8 + near) * 8 + y
+
+
+EIGHT, FOUR, TWO = range(8), range(4), range(2)
+FIRST = [[device(2 * z + k, n, y) for k in TWO for n in EIGHT] for z in FOUR for y in EIGHT]
+SECOND = [
+    [device(2 * z + k, n, 2 * y + m) for z in FOUR for y in FOUR]
+    for k in TWO
+    for n in EIGHT
+    for m in TWO
+]
+THIRD = [[device(z, n, 2 * y + m) for m in TWO for n in EIGHT] for z in EIGHT for y in FOUR]
 
 
 WIDTH = 384
@@ -18,6 +31,7 @@
 CELLS_R = 8
 CELLS_C = 32
 HID = 1536
+HALF = 16
 
 
 def taps(acc, rows, weight_ref, lanes, b, first):
@@ -126,7 +140,7 @@
         ).astype(jnp.bfloat16)
 
 
-def rows_kernel(acc_in, low_ref, high_ref, weight_ref, acc_ref, wide):
+def halo_rows(acc_in, low_ref, high_ref, weight_ref, acc_ref, wide):
     for c in range(3):
         lanes = pl.ds(c * LANES, LANES)
         wide[c, :, 0:8, :] = jnp.zeros((6, 8, LANES), jnp.float32)
@@ -150,8 +164,99 @@
     lax.fori_loop(0, 3, lane_tile, 0)
 
 
+def halo_columns(acc_ref, left_ref, right_ref, weight_ref, edge):
+    tall = CELLS_R + 6
+    edge[...] = jnp.zeros(edge.shape, jnp.float32)
+    for c in range(3):
+        lanes = pl.ds(c * LANES, LANES)
+        edge[0, c, :, 5:8, :] = left_ref[:, :, lanes].astype(jnp.float32)
+        edge[1, c, :, 8:11, :] = right_ref[:, :, lanes].astype(jnp.float32)
+
+    def lane_tile(c, carry):
+        lanes = pl.ds(pl.multiple_of(c * LANES, LANES), LANES)
+        for side in (0, 1):
+            here = slice(8 * side, 8 * side + 8)
+            acc = [acc_ref[i, here, lanes] for i in range(CELLS_R)]
+            for b in (0, 1, 2) if side == 0 else (4, 5, 6):
+                at = 5 + b if side == 0 else b - 3
+                rows = [edge[side, c, r, at : at + 8, :] for r in range(tall)]
+                acc = taps(acc, rows, weight_ref, lanes, b, -3)
+            for i in range(CELLS_R):
+                acc_ref[i, here, lanes] = acc[i]
+        return carry
+
+    lax.fori_loop(0, 3, lane_tile, 0)
+
+
 def gelu(x):
     return 0.5 * x * (1.0 + lax.erf(x * (0.5**0.5)))
+
+
+def block_of(conv_rows, inputs, lines_ref, expand_ref, shrink_ref, normed, hidden):
+    gain, norm_bias, shrink_bias, scale = (lines_ref[k : k + 1, :] for k in range(4))
+    for i in range(CELLS_R):
+        conv = conv_rows(i)
+        center = jnp.mean(conv, axis=-1, keepdims=True)
+        conv = conv - center
+        variance = jnp.mean(conv * conv, axis=-1, keepdims=True)
+        normed[i * HALF : (i + 1) * HALF, :] = (
+            conv * lax.rsqrt(variance + 1e-06) * gain + norm_bias
+        ).astype(jnp.bfloat16)
+    for k in range(HID // WIDTH):
+        lanes = slice(k * WIDTH, (k + 1) * WIDTH)
+        part = jnp.dot(normed[...], expand_ref[:, lanes], preferred_element_type=jnp.float32)
+        hidden[:, lanes] = gelu(part + lines_ref[4 + k : 5 + k, :]).astype(jnp.bfloat16)
+    shrunk = jnp.dot(hidden[...], shrink_ref[...], preferred_element_type=jnp.float32)
+    shrunk = shrunk + shrink_bias
+    inputs = inputs.reshape(CELLS_R * HALF, WIDTH).astype(jnp.float32)
+    return (inputs + scale * shrunk).astype(jnp.bfloat16)
+
+
+def keys_of(block, key_ref):
+    return jnp.dot(block, key_ref[...], preferred_element_type=jnp.float32).astype(jnp.bfloat16)
+
+
+def values_of(block, turned_ref):
+    return lax.dot_general(
+        turned_ref[...], block, (((1,), (1,)), ((), ())), preferred_element_type=jnp.float32
+    ).astype(jnp.bfloat16)
+
+
+def inner_kernel(
+    acc_in,
+    low_ref,
+    high_ref,
+    weight_ref,
+    x_ref,
+    lines_ref,
+    expand_ref,
+    shrink_ref,
+    key_ref,
+    turned_ref,
+    sides_ref,
+    block_ref,
+    keys_ref,
+    values_ref,
+    wide,
+    acc_ref,
+    normed,
+    hidden,
+):
+    halo_rows(acc_in, low_ref, high_ref, weight_ref, acc_ref, wide)
+    sides_ref[:, 0:8, :] = acc_ref[:, 0:8, :]
+    sides_ref[:, 8:16, :] = acc_ref[:, CELLS_C - 8 : CELLS_C, :]
+    block = block_of(
+        lambda i: acc_ref[i, 8 : 8 + HALF, :],
+        x_ref[:, 8 : 8 + HALF, :],
+        lines_ref,
+        expand_ref,
+        shrink_ref,
+        normed,
+        hidden,
+    )
+    block_ref[...] = block.reshape(CELLS_R, HALF, WIDTH)
+    keys_ref[...] = keys_of(block, key_ref)
+    values_ref[...] = values_of(block, turned_ref)
 
 
 def marked(weighted, marks):
@@ -163,72 +268,54 @@
     return jnp.concatenate([weighted, marks], axis=1).astype(jnp.bfloat16)
 
 
-def cells_kernel(
+def outer_kernel(
     tissue_ref,
-    acc_ref,
+    acc_in,
     left_ref,
     right_ref,
     weight_ref,
     x_ref,
-    rows_ref,
+    lines_ref,
     expand_ref,
     shrink_ref,
     key_ref,
     turned_ref,
     big_ref,
+    block_ref,
+    keys_ref,
+    values_ref,
     out_ref,
     part_ref,
+    acc_ref,
     edge,
     normed,
     hidden,
     sums,
+    whole,
+    sem,
 ):
-    count = CELLS_R * CELLS_C
-    tall = CELLS_R + 6
-    edge[...] = jnp.zeros(edge.shape, jnp.float32)
-    for c in range(3):
-        lanes = pl.ds(c * LANES, LANES)
-        edge[0, c, :, 5:8, :] = left_ref[:, :, lanes].astype(jnp.float32)
-        edge[1, c, :, 8:11, :] = right_ref[:, :, lanes].astype(jnp.float32)
-
-    def lane_tile(c, carry):
-        lanes = pl.ds(pl.multiple_of(c * LANES, LANES), LANES)
-        for side, j in ((0, 0), (1, CELLS_C // 8 - 1)):
-            acc = [acc_ref[i, 8 * j : 8 * j + 8, lanes] for i in range(CELLS_R)]
-            for b in (0, 1, 2) if side == 0 else (4, 5, 6):
-                at = 5 + b if side == 0 else b - 3
-                rows = [edge[side, c, r, at : at + 8, :] for r in range(tall)]
-                acc = taps(acc, rows, weight_ref, lanes, b, -3)
-            for i in range(CELLS_R):
-                acc_ref[i, 8 * j : 8 * j + 8, lanes] = acc[i]
-        return carry
-
-    lax.fori_loop(0, 3, lane_tile, 0)
-    gain, norm_bias, shrink_bias, scale = (rows_ref[k : k + 1, :] for k in range(4))
-    for i in range(CELLS_R):
-        conv = acc_ref[i]
-        center = jnp.mean(conv, axis=-1, keepdims=True)
-        conv = conv - center
-        variance = jnp.mean(conv * conv, axis=-1, keepdims=True)
-        normed[i * CELLS_C : (i + 1) * CELLS_C, :] = (
-            conv * lax.rsqrt(variance + 1e-06) * gain + norm_bias
-        ).astype(jnp.bfloat16)
-    for k in range(HID // WIDTH):
-        lanes = slice(k * WIDTH, (k + 1) * WIDTH)
-        part = jnp.dot(normed[...], expand_ref[:, lanes], preferred_element_type=jnp.float32)
-        hidden[:, lanes] = gelu(part + rows_ref[4 + k : 5 + k, :]).astype(jnp.bfloat16)
-    shrunk = jnp.dot(hidden[...], shrink_ref[...], preferred_element_type=jnp.float32)
-    shrunk = shrunk + shrink_bias
-    block = (x_ref[...].reshape(count, WIDTH).astype(jnp.float32) + scale * shrunk).astype(
-        jnp.bfloat16
-    )
-    out_ref[...] = block.reshape(CELLS_R, CELLS_C, WIDTH)
-    keys = jnp.dot(block, key_ref[...], preferred_element_type=jnp.float32).astype(jnp.bfloat16)
-    values = lax.dot_general(
-        turned_ref[...], block, (((1,), (1,)), ((), ())), preferred_element_type=jnp.float32
-    ).astype(jnp.bfloat16)
+    acc_ref[...] = acc_in[...]
+    whole[:, 8 : 8 + HALF, :] = block_ref[...]
+    halo_columns(acc_ref, left_ref, right_ref, weight_ref, edge)
+    block = block_of(
+        lambda i: acc_ref[i],
+        jnp.concatenate([x_ref[:, 0:8, :], x_ref[:, CELLS_C - 8 : CELLS_C, :]], axis=1),
+        lines_ref,
+        expand_ref,
+        shrink_ref,
+        normed,
+        hidden,
+    )
+    parts = block.reshape(CELLS_R, HALF, WIDTH)
+    whole[:, 0:8, :] = parts[:, 0:8, :]
+    whole[:, CELLS_C - 8 : CELLS_C, :] = parts[:, 8:16, :]
+    copy = pltpu.make_async_copy(whole, out_ref, sem)
+    copy.start()
+    keys = jnp.concatenate([keys_ref[...], keys_of(block, key_ref)], axis=0)
+    values = jnp.concatenate([values_ref[...], values_of(block, turned_ref)], axis=1)
     size = WIDTH // NH
-    groups = CELLS_C // TILE
+    tiles = ((1, 2), (0, 3))
+    live = [[tissue_ref[0, t] > 0 for t in pair] for pair in tiles]
     line = lax.broadcasted_iota(jnp.int32, (NH, LANES), 0)
     tops = jnp.zeros((NH, LANES), jnp.float32)
     totals = jnp.zeros((NH, LANES), jnp.float32)
@@ -236,36 +323,41 @@
         scores = jnp.dot(
             keys, big_ref[:, t * LANES : (t + 1) * LANES], preferred_element_type=jnp.float32
         ) * (size**-0.5 * LOG2E)
-        scores = scores.reshape(CELLS_R, groups, TILE, LANES)
-        scores = [jnp.where(tissue_ref[0, g] > 0, scores[:, g], -1e30) for g in range(groups)]
-        top = scores[0]
-        for g in range(1, groups):
-            top = jnp.maximum(top, scores[g])
+        scores = scores.reshape(2, CELLS_R, 2, TILE, LANES)
+        scores = [
+            [jnp.where(live[h][g], scores[h, :, g], -1e30) for g in range(2)] for h in range(2)
+        ]
+        top = jnp.maximum(
+            jnp.maximum(scores[0][0], scores[0][1]), jnp.maximum(scores[1][0], scores[1][1])
+        )
         top = jnp.ceil(jnp.max(jnp.max(top, axis=0), axis=0, keepdims=True))
         weights = [
-            jnp.where(tissue_ref[0, g] > 0, jnp.exp2(scores[g] - top), 0.0) for g in range(groups)
+            [jnp.where(live[h][g], jnp.exp2(scores[h][g] - top), 0.0) for g in range(2)]
+            for h in range(2)
         ]
-        total = weights[0]
-        for g in range(1, groups):
-            total = total + weights[g]
+        total = (weights[0][0] + weights[0][1]) + (weights[1][0] + weights[1][1])
         total = jnp.sum(jnp.sum(total, axis=0), axis=0, keepdims=True)
-        weights = jnp.stack(weights, axis=1).reshape(count, LANES).astype(jnp.bfloat16)
+        weights = [jnp.stack(pair, axis=1).reshape(CELLS_R * HALF, LANES) for pair in weights]
+        weights = jnp.concatenate(weights, axis=0).astype(jnp.bfloat16)
         pair = jnp.dot(
             values[2 * size * t : 2 * size * (t + 1), :], weights, preferred_element_type=jnp.float32
         )
         sums[2 * size * t : 2 * size * t + size, :] = pair[:size]
         sums[2 * size * t + size : 2 * size * (t + 1), :] = pltpu.roll(pair[size:], NQ, 1)
+        top = jnp.broadcast_to(top, (NH, LANES))
+        total = jnp.broadcast_to(total, (NH, LANES))
         tops = jnp.where(line == 2 * t, top, tops)
-        tops = jnp.where(line == 2 * t + 1, pltpu.roll(jnp.broadcast_to(top, (NH, LANES)), NQ, 1), tops)
+        tops = jnp.where(line == 2 * t + 1, pltpu.roll(top, NQ, 1), tops)
         totals = jnp.where(line == 2 * t, total, totals)
-        totals = jnp.where(
-            line == 2 * t + 1, pltpu.roll(jnp.broadcast_to(total, (NH, LANES)), NQ, 1), totals
-        )
+        totals = jnp.where(line == 2 * t + 1, pltpu.roll(total, NQ, 1), totals)
     sums[WIDTH:, :] = jnp.zeros((LANES, LANES), jnp.float32)
     sums[WIDTH : WIDTH + NH, :] = tops
     sums[WIDTH + 3 * NH : WIDTH + 4 * NH, :] = totals
     part = sums[...].T
-    part_ref[...] = marked(part[:NQ, :WIDTH], part[:NQ, WIDTH:])
+    part_ref[...] = jnp.broadcast_to(
+        marked(part[:NQ, :WIDTH], part[:NQ, WIDTH:])[None], part_ref.shape
+    )
+    copy.wait()
 
 
 def spread_matrix(first, copies):
@@ -298,19 +390,19 @@
     out_ref[...] = jnp.broadcast_to(part[None], out_ref.shape)
 
 
-def pool_kernel(parts_ref, out_ref):
-    weighted, _, total, inside = combined(parts_ref[...])
+def pool_kernel(parts_ref, class_ref, label_ref, out_ref, loss_ref):
+    weighted, _, total, inside = combined(parts_ref[...].reshape(2, NQ, WIDTH + LANES))
     marks = marked(weighted, jnp.where(inside, 1.0 / total, 0.0))[:, WIDTH:]
     inverse = jnp.dot(marks, spread_matrix(3 * NH, 3), preferred_element_type=jnp.float32)
-    out_ref[...] = jnp.broadcast_to((weighted * inverse)[None], out_ref.shape)
-
-
-def loss_kernel(pooled_ref, class_ref, label_ref, out_ref, loss_ref):
-    pooled = pooled_ref[...]
+    pooled = weighted * inverse
     out_ref[...] = pooled
     lines = jnp.sum(pooled.reshape(NQ // 8, 8, WIDTH), axis=0)
-    logits = jnp.dot(
-        lines, class_ref[...], precision=lax.Precision.HIGHEST, preferred_element_type=jnp.float32
+    logits = lax.dot_general(
+        lines,
+        class_ref[...],
+        (((1,), (1,)), ((), ())),
+        precision=lax.Precision.HIGHEST,
+        preferred_element_type=jnp.float32,
     )
     logits = jnp.sum(logits, axis=0, keepdims=True)
     label = label_ref[...].reshape(logits.shape).astype(jnp.float32)
@@ -318,8 +410,8 @@
     loss_ref[0] = jnp.sum(soft - label * logits)
 
 
-def everyone(part, axis, groups=None):
-    return lax.all_to_all(part, axis, 0, 0, axis_index_groups=groups, tiled=True)
+def everyone(part, groups):
+    return lax.all_to_all(part, ("row", "col"), 0, 0, axis_index_groups=groups, tiled=True)
 
 
 def call(kernel, out_shape, name, *args, **more):
@@ -327,19 +419,17 @@
 
 
 def merged(part, class_weight, slide_label):
-    chunk = (8, NQ // 8, WIDTH + LANES)
+    chunk = (16, NQ // 8, WIDTH + LANES)
     same = jax.ShapeDtypeStruct(chunk, jnp.bfloat16)
-    parts = everyone(part.reshape(chunk), "row", NEAR)
-    parts = everyone(call(merge_kernel, same, "merge_near", parts), "row", FAR)
-    parts = everyone(call(merge_kernel, same, "merge_far", parts), "col")
-    rows = jax.ShapeDtypeStruct((8, NQ // 8, WIDTH), jnp.float32)
-    pooled = everyone(call(pool_kernel, rows, "pool", parts), "row", NEAR)
+    parts = everyone(part.reshape(chunk), FIRST)
+    parts = everyone(call(merge_kernel, same, "merge_first", parts), SECOND)
+    parts = everyone(call(merge_kernel, same, "merge_second", parts), THIRD)
     return call(
-        loss_kernel,
+        pool_kernel,
         (jax.ShapeDtypeStruct((NQ, WIDTH), jnp.float32), jax.ShapeDtypeStruct((1,), jnp.float32)),
-        "loss",
-        pooled.reshape(NQ, WIDTH),
-        class_weight,
+        "pool",
+        parts,
+        class_weight.T,
         slide_label,
         out_specs=(pl.BlockSpec(memory_space=pltpu.VMEM), pl.BlockSpec(memory_space=pltpu.SMEM)),
     )
@@ -357,10 +447,12 @@
 
 
 def exchanged(first, last, axis):
-    count = lax.axis_size(axis)
-    forward = [(i, i + 1) for i in range(count - 1)]
-    backward = [(target, source) for source, target in forward]
-    return lax.ppermute(last, axis, forward), lax.ppermute(first, axis, backward)
+    count, odd = lax.axis_size(axis), lax.axis_index(axis) % 2 == 1
+    inner = [(i, i ^ 1) for i in range(count)]
+    outer = [(i, i + 1 if i % 2 else i - 1) for i in range(1, count - 1)]
+    near = lax.ppermute(jnp.where(odd, first, last), axis, inner)
+    far = lax.ppermute(jnp.where(odd, last, first), axis, outer)
+    return jnp.where(odd, near, far), jnp.where(odd, far, near)
 
 
 def per_device(
@@ -436,23 +528,35 @@
         jnp.concatenate([low[:, -3:], last, high[:, -3:]], axis=0),
         "col",
     )
-    acc = call(
-        rows_kernel,
-        shaped((rows, cols, width), f32),
-        "halo_rows",
+    count = rows * HALF
+    work = [pltpu.VMEM((count, width), bf16), pltpu.VMEM((count, HID), bf16)]
+    sides, inner, keys, values = call(
+        inner_kernel,
+        (
+            shaped((rows, HALF, width), f32),
+            shaped((rows, HALF, width), bf16),
+            shaped((count, width), bf16),
+            shaped((width, count), bf16),
+        ),
+        "inner_cells",
         acc,
         low,
         high,
         taps_,
-        scratch_shapes=[vmem(3, 6, cols + 16, LANES)],
-        input_output_aliases={0: 0},
+        cells,
+        lines,
+        expand,
+        shrink,
+        key,
+        turned,
+        scratch_shapes=[vmem(3, 6, cols + 16, LANES), vmem(rows, cols, width), *work],
     )
     block_out, part = call(
-        cells_kernel,
-        (shaped((rows, cols, width), bf16), shaped((NQ, width + LANES), bf16)),
-        "cells",
+        outer_kernel,
+        (shaped((rows, cols, width), bf16), shaped((2, NQ, width + LANES), bf16)),
+        "outer_cells",
         tissue,
-        acc,
+        sides,
         left,
         right,
         taps_,
@@ -463,12 +567,18 @@
         key,
         turned,
         big,
-        in_specs=[pl.BlockSpec(memory_space=pltpu.SMEM)] + [whole] * 11,
+        inner,
+        keys,
+        values,
+        in_specs=[pl.BlockSpec(memory_space=pltpu.SMEM)] + [whole] * 14,
+        out_specs=(hbm, whole),
         scratch_shapes=[
+            vmem(rows, HALF, width),
             vmem(2, 3, rows + 6, 16, LANES),
-            pltpu.VMEM((rows * cols, width), bf16),
-            pltpu.VMEM((rows * cols, HID), bf16),
+            *work,
             vmem(width + LANES, LANES),
+            pltpu.VMEM((rows, cols, width), bf16),
+            pltpu.SemaphoreType.DMA,
         ],
     )
     pooled, slide_loss = merged(part, class_weight, slide_label)

time: 80.9 us -> 73.1 us (0.904)
  waiting for transfers between devices: 8.36 us -> 0.58 us
  blocking collectives: 41.5 us -> 48.5 us
  starting transfers between devices: 19.6 us -> 12.8 us
  local copies, waits for them, and re-layouts: 1.1 us -> 0.04 us
  other arithmetic: 0.08 us -> 1.08 us
    all_to_all x3, blocking collectives: 41.5 us -> 48.5 us  [everyone(): lax.all_to_all(part, ('row', 'col'), 0, 0, axis_index_groups=groups, tile...]
    all_to_all x1 -> x0, starting transfers between devices: 6.89 us -> none  [everyone(): lax.all_to_all(part, axis, 0, 0, axis_index_groups=groups, tiled=True)]
    all_to_all x1 -> x0, waiting for transfers between devices: 4.87 us -> none  [everyone(): lax.all_to_all(part, axis, 0, 0, axis_index_groups=groups, tiled=True)]
    ppermute x4, waiting for transfers between devices: 3.49 us -> 0.58 us  [the longest x2 0.58 us: exchanged(): near = lax.ppermute(jnp.where(odd, first, last), axis, inner)]
    select_n x0 -> x4, other arithmetic: none -> 1.08 us  [the longest x2 1.02 us: exchanged(): far = lax.ppermute(jnp.where(odd, last, first), axis, outer)]
    slice x2 -> x0, local copies, waits for them, and re-layouts: 0.95 us -> none  [the longest x1 0.94 us: per_device(): low, high = exchanged(features[:3], features[-3:], 'row')]
    pallas_call x7 -> x6, Pallas kernels: 9.11 us -> 8.89 us  [call(): pl.pallas_call(kernel, out_shape=out_shape, name=name, **more, **params())]
  transfers between devices with their start and end apart: 5 -> 4, of which waited for: 2 -> 1; matrix products, arithmetic and copies ran while one was open for 0% -> 0% of each run, Pallas kernels for 4% -> 6%
where the time goes in v2:
time: 73.1 us; the launch traced here: 72.7 us
  blocking collectives  48.5 us (66%)
  starting transfers between devices  12.8 us (18%)
  Pallas kernels  8.89 us (12%)
  other arithmetic  1.08 us (1%)
  between operations  0.8 us (1%)
    all_to_all x3, blocking collectives, everyone(): lax.all_to_all(part, ('row', 'col'), 0, 0, axis_index_groups=groups, tile...  48.5 us
    pallas_call x6, Pallas kernels, call(): pl.pallas_call(kernel, out_shape=out_shape, name=name, **more, **params())  8.89 us
    ppermute x2, starting transfers between devices, exchanged(): near = lax.ppermute(jnp.where(odd, first, last), axis, inner)  7.67 us
    ppermute x2, starting transfers between devices, exchanged(): far = lax.ppermute(jnp.where(odd, last, first), axis, outer)  5.17 us
  transfers between devices with their start and end apart: 4, of which 1 were waited for; matrix products, arithmetic and copies ran while one was open for 0% of the time, Pallas kernels for 6%

profile of v2, /device:TPU:1, one launch (start us, length us, event | category | flops | bytes accessed | tf_op | source)
XLA Modules:
  0.0 72.7 jit_solution(16907274999956035266)
XLA Ops:
  0.6 0.9 %broadcast_select_fusion.2 = (bf16[3,32,384]{2,1,0:T(8,128)(2,1)S(1)}, bf16[3,32,384]{2,1,0:T(8,128)(2,1)S(1)}) fusion(pred[]{:T(512)S(6)} %eq.9, bf16[8,32,384]{2,1,0:T(8,128)(2,1)} %x_hbm.1), kind=kLoop, calls=%fused_computation.2 | loop fusion | flops 73728 | bytes 294913 | tf_op jit(solution)/shard_map/jit(_where)/select_n | solution.py:454
  1.6 4.5 %collective-permute-start.1 = (bf16[3,32,384]{2,1,0:T(8,128)(2,1)S(1)}, bf16[3,32,384]{2,1,0:T(8,128)(2,1)S(1)}, u32[]{:S(2)}, u32[]{:S(2)}) collective-permute-start(bf16[3,32,384]{2,1,0:T(8,128)(2,1)S(1)} %get-tuple-element.41), channel_id=1, source_target_pairs={{8,16},{16,8},{24,32},{32,24},{40,48},{48,40},{56,64},{64,56},{72,... | collective-permute-start | bytes 221192 | tf_op jit(solution)/shard_map/ppermute | solution.py:454
  6.1 4.9 %collective-permute-start = (bf16[3,32,384]{2,1,0:T(8,128)(2,1)S(1)}, bf16[3,32,384]{2,1,0:T(8,128)(2,1)S(1)}, u32[]{:S(2)}, u32[]{:S(2)}) collective-permute-start(bf16[3,32,384]{2,1,0:T(8,128)(2,1)S(1)} %get-tuple-element.42), channel_id=1, source_target_pairs={{0,8},{8,0},{16,24},{24,16},{32,40},{40,32},{48,56},{56,48},{64,72... | collective-permute-start | bytes 221192 | tf_op jit(solution)/shard_map/ppermute | solution.py:453
  11.1 2.6 %own_cells.1 = (f32[8,32,384]{2,1,0:T(8,128)S(1)}, bf16[8,3,384]{2,1,0:T(4,128)(2,1)S(1)}, bf16[8,3,384]{2,1,0:T(4,128)(2,1)S(1)}, bf16[8,32,384]{2,1,0:T(8,128)...) custom-call(bf16[8,32,384]{2,1,0:T(8,128)(2,1)} %x_hbm.1, ...), custom_call_target="tpu_custom_call" | custom-call | flops 1000000 | bytes 1000000 | tf_op jit(solution)/shard_map/own_cells/pallas_call | solution.py:418
  13.7 0.0 collective-permute-done.1
  13.7 0.0 collective-permute-done
  13.7 0.1 broadcast_select_fusion.6
  13.8 0.7 collective-permute-start.3
  14.5 2.7 %collective-permute-start.2 = (bf16[14,3,384]{2,1,0:T(4,128)(2,1)S(1)}, bf16[14,3,384]{2,1,0:T(4,128)(2,1)S(1)}, u32[]{:S(2)}, u32[]{:S(2)}) collective-permute-start(bf16[14,3,384]{2,1,0:T(4,128)(2,1)S(1)} %get-tuple-element.48), channel_id=1, source_target_pairs={{0,1},{1,0},{2,3},{3,2},{4,5},{5,4},{6,7},{7,6},{8,9},{9,8},{10,11... | collective-permute-start | bytes 96776 | tf_op jit(solution)/shard_map/ppermute | solution.py:453
  17.2 0.0 copy-start.1
  17.2 1.4 %inner_cells.1 = (f32[8,16,384]{2,1,0:T(8,128)S(1)}, bf16[8,16,384]{2,1,0:T(8,128)(2,1)S(1)}, bf16[128,384]{1,0:T(8,128)(2,1)S(1)}, bf16[384,128]{1,0:T(8,128)(2,1)S(1)}) custom-call(f32[8,32,384]{2,1,0:T(8,128)S(1)} %get-tuple-element.22.acc_in, bf16[3,32,384]{2,1,0:T(8,128)(2,1)S(1)} %get-tuple-element.44.low_ref, ...), custom_call_target="tpu_custom_call" | custom-call | flops 1000000 | bytes 1000000 | tf_op jit(solution)/shard_map/inner_cells/pallas_call | solution.py:418
  18.7 0.0 collective-permute-done.3
  18.7 0.6 collective-permute-done.2
  19.3 0.0 copy-done.1
  19.3 3.1 %outer_cells.1 = (bf16[8,32,384]{2,1,0:T(8,128)(2,1)}, bf16[2,64,512]{2,1,0:T(8,128)(2,1)S(1)}) custom-call(s32[1,4]{1,0:T(1,128)S(1)} %copy-done.1, f32[8,16,384]{2,1,0:T(8,128)S(1)} %get-tuple-element.30.acc_in, bf16[14,3,384]{2,1,0:T(4,128)(2,1)S(1)} %get-tuple-element.46.left_ref, bf16[14,3,384]{2,1,0:T(4,128)(2,1)S(1)} %get-tuple-element.45.right_ref, ...), custom_call_target="tpu_custom_call" | custom-call | flops 1000000 | bytes 1000000 | tf_op jit(solution)/shard_map/outer_cells/pallas_call | solution.py:418
  22.4 0.0 copy-start
  22.5 0.0 copy-start.2
  22.5 13.6 %all_to_all.15.parts_ref = bf16[16,8,512]{2,1,0:T(8,128)(2,1)S(1)} all-to-all(bf16[16,8,512]{2,1,0:T(8,128)(2,1)S(1)} %bitcast.2), channel_id=1, replica_groups={{0,8,16,24,32,40,48,56,64,72,80,88,96,104,112,120},{1,9,17,25,33,41,49,..., dimensions={0} | all-to-all | bytes 262144 | tf_op jit(solution)/shard_map/all_to_all | solution.py:414
  36.0 0.3 merge_first.1
  36.3 24.2 %all_to_all.16.parts_ref = bf16[16,8,512]{2,1,0:T(8,128)(2,1)S(1)} all-to-all(bf16[16,8,512]{2,1,0:T(8,128)(2,1)S(1)} %merge_first.1), channel_id=1, replica_groups={{0,2,4,6,128,130,132,134,256,258,260,262,384,386,388,390},{1,3,5,7,129,..., dimensions={0} | all-to-all | bytes 262144 | tf_op jit(solution)/shard_map/all_to_all | solution.py:414
  60.5 0.3 merge_second.1
  60.8 10.7 %all_to_all.17.parts_ref = bf16[16,8,512]{2,1,0:T(8,128)(2,1)S(1)} all-to-all(bf16[16,8,512]{2,1,0:T(8,128)(2,1)S(1)} %merge_second.1), channel_id=1, replica_groups={{0,8,16,24,32,40,48,56,1,9,17,25,33,41,49,57},{2,10,18,26,34,42,50,58,3..., dimensions={0} | all-to-all | bytes 262144 | tf_op jit(solution)/shard_map/all_to_all | solution.py:414
  71.5 0.0 copy-done
  71.5 0.0 copy-done.2
  71.5 1.2 %pool.1 = (f32[64,384]{1,0:T(8,128)}, f32[1]{0:T(128)}) custom-call(bf16[16,8,512]{2,1,0:T(8,128)(2,1)S(1)} %all_to_all.17.parts_ref, f32[16,384]{1,0:T(8,128)S(1)} %bitcast.3, s32[16]{0:T(128)S(1)} %copy-done.2), custom_call_target="tpu_custom_call" | custom-call | flops 1000000 | bytes 1000000 | tf_op jit(solution)/shard_map/pool/pallas_call | solution.py:418
  (3 shorter events, 0.1 us)
Async XLA Ops:
  1.6 12.1 %collective-permute-start.1 = (bf16[3,32,384]{2,1,0:T(8,128)(2,1)S(1)}, bf16[3,32,384]{2,1,0:T(8,128)(2,1)S(1)}, u32[]{:S(2)}, u32[]{:S(2)}) collective-permute-start(bf16[3,32,384]{2,1,0:T(8,128)(2,1)S(1)} %get-tuple-element.41), channel_id=1, source_target_pairs={{8,16},{16,8},{24,32},{32,24},{40,48},{48,40},{56,64},{64,56},{72,... | collective-permute-start | bytes 221192 | tf_op jit(solution)/shard_map/ppermute | solution.py:454
  6.1 7.6 %collective-permute-start = (bf16[3,32,384]{2,1,0:T(8,128)(2,1)S(1)}, bf16[3,32,384]{2,1,0:T(8,128)(2,1)S(1)}, u32[]{:S(2)}, u32[]{:S(2)}) collective-permute-start(bf16[3,32,384]{2,1,0:T(8,128)(2,1)S(1)} %get-tuple-element.42), channel_id=1, source_target_pairs={{0,8},{8,0},{16,24},{24,16},{32,40},{40,32},{48,56},{56,48},{64,72... | collective-permute-start | bytes 221192 | tf_op jit(solution)/shard_map/ppermute | solution.py:453
  13.8 4.9 %collective-permute-start.3 = (bf16[14,3,384]{2,1,0:T(4,128)(2,1)S(1)}, bf16[14,3,384]{2,1,0:T(4,128)(2,1)S(1)}, u32[]{:S(2)}, u32[]{:S(2)}) collective-permute-start(bf16[14,3,384]{2,1,0:T(4,128)(2,1)S(1)} %get-tuple-element.47), channel_id=1, source_target_pairs={{1,2},{2,1},{3,4},{4,3},{5,6},{6,5},{9,10},{10,9},{11,12},{12,11},... | collective-permute-start | bytes 96776 | tf_op jit(solution)/shard_map/ppermute | solution.py:454
  14.5 4.8 %collective-permute-start.2 = (bf16[14,3,384]{2,1,0:T(4,128)(2,1)S(1)}, bf16[14,3,384]{2,1,0:T(4,128)(2,1)S(1)}, u32[]{:S(2)}, u32[]{:S(2)}) collective-permute-start(bf16[14,3,384]{2,1,0:T(4,128)(2,1)S(1)} %get-tuple-element.48), channel_id=1, source_target_pairs={{0,1},{1,0},{2,3},{3,2},{4,5},{5,4},{6,7},{7,6},{8,9},{9,8},{10,11... | collective-permute-start | bytes 96776 | tf_op jit(solution)/shard_map/ppermute | solution.py:453
  17.2 2.1 %copy-start.1 = (s32[1,4]{1,0:T(1,128)S(1)}, s32[1,4]{1,0:T(1,128)}, u32[]{:S(2)}) copy-start(s32[1,4]{1,0:T(1,128)} %tissue_ref.1) | copy-start | bytes 52
  22.4 49.1 %copy-start = (f32[384,16]{0,1:T(8,128)S(1)}, f32[384,16]{0,1:T(8,128)}, u32[]{:S(2)}) copy-start(f32[384,16]{0,1:T(8,128)} %param.29) | copy-start | bytes 73732
  22.5 49.1 %copy-start.2 = (s32[16]{0:T(128)S(1)}, s32[16]{0:T(128)}, u32[]{:S(2)}) copy-start(s32[16]{0:T(128)} %label_ref.1) | copy-start | bytes 196

commit v3 on v2

--- a/solution.py
+++ b/solution.py
@@ -44,35 +44,44 @@
     return acc
 
 
+def fetch_kernel(
+    x_hbm, weight_hbm, bias_hbm, x_ref, weight_ref, bias_ref, inner_ref, outer_ref, first_ref, last_ref, sems
+):
+    pairs = ((x_hbm, x_ref), (weight_hbm, weight_ref), (bias_hbm, bias_ref))
+    copies = [pltpu.make_async_copy(s, d, sems.at[k]) for k, (s, d) in enumerate(pairs)]
+    for copy in copies:
+        copy.start()
+    copies[0].wait()
+    odd = lax.axis_index("row") % 2
+    inner_ref[...] = x_ref[pl.ds((1 - odd) * (CELLS_R - 3), 3)]
+    outer_ref[...] = x_ref[pl.ds(odd * (CELLS_R - 3), 3)]
+    first_ref[...] = x_ref[:, 0:3, :]
+    last_ref[...] = x_ref[:, CELLS_C - 3 : CELLS_C, :]
+    for copy in copies[1:]:
+        copy.wait()
+
+
 def own_kernel(
-    x_hbm,
-    weight_hbm,
+    x_ref,
+    weight_ref,
+    bias_ref,
     expand_hbm,
-    shrink_hbm,
     key_hbm,
     value_hbm,
     query_hbm,
-    bias_hbm,
     gain_hbm,
     norm_bias_hbm,
     shrink_bias_hbm,
     scale_hbm,
     expand_bias_hbm,
     acc_ref,
-    first_ref,
-    last_ref,
-    x_ref,
-    weight_ref,
     expand_ref,
-    shrink_ref,
     key_ref,
     turned_ref,
-    big_ref,
+    query_ref,
     rows_ref,
     wide,
     value_ref,
-    query_ref,
-    bias_ref,
     gain_ref,
     norm_bias_ref,
     shrink_bias_ref,
@@ -81,28 +90,23 @@
     sems,
 ):
     pairs = (
-        (x_hbm, x_ref),
-        (weight_hbm, weight_ref),
-        (bias_hbm, bias_ref),
-        (query_hbm, query_ref),
-        (value_hbm, value_ref),
         (gain_hbm, gain_ref),
         (norm_bias_hbm, norm_bias_ref),
         (shrink_bias_hbm, shrink_bias_ref),
         (scale_hbm, scale_ref),
         (expand_bias_hbm, expand_bias_ref),
+        (query_hbm, query_ref),
+        (value_hbm, value_ref),
         (key_hbm, key_ref),
-        (expand_hbm, expand_ref),
-        (shrink_hbm, shrink_ref),
+        *(
+            (expand_hbm.at[k : k + LANES], expand_ref.at[k : k + LANES])
+            for k in range(0, WIDTH, LANES)
+        ),
     )
     copies = [pltpu.make_async_copy(s, d, sems.at[k]) for k, (s, d) in enumerate(pairs)]
     for copy in copies:
         copy.start()
-    for copy in copies[:3]:
-        copy.wait()
     rows_ref[8:9, :] = bias_ref[...].reshape(1, WIDTH)
-    first_ref[...] = x_ref[:, 0:3, :]
-    last_ref[...] = x_ref[:, CELLS_C - 3 : CELLS_C, :]
     for c in range(3):
         lanes = pl.ds(c * LANES, LANES)
         wide[c, :, 0:8, :] = jnp.zeros((CELLS_R, 8, LANES), jnp.float32)
@@ -123,21 +127,13 @@
         return carry
 
     lax.fori_loop(0, 3, lane_tile, 0)
-    for copy in copies[3:]:
+    for copy in copies:
         copy.wait()
+    turned_ref[...] = value_ref[...].astype(jnp.float32).T.astype(jnp.bfloat16)
     for row, ref in enumerate((gain_ref, norm_bias_ref, shrink_bias_ref, scale_ref)):
         rows_ref[row : row + 1, :] = ref[...].reshape(1, WIDTH)
     for k in range(HID // WIDTH):
         rows_ref[4 + k : 5 + k, :] = expand_bias_ref[k * WIDTH : (k + 1) * WIDTH].reshape(1, WIDTH)
-    turned_ref[...] = value_ref[...].astype(jnp.float32).T.astype(jnp.bfloat16)
-    query = query_ref[...].astype(jnp.float32)
-    query = jnp.concatenate([query, query], axis=0).T
-    head = lax.broadcasted_iota(jnp.int32, (WIDTH, LANES), 0) // (WIDTH // NH)
-    half = lax.broadcasted_iota(jnp.int32, (WIDTH, LANES), 1) // NQ
-    for t in range(NH // 2):
-        big_ref[:, t * LANES : (t + 1) * LANES] = jnp.where(
-            head == 2 * t + half, query, 0.0
-        ).astype(jnp.bfloat16)
 
 
 def halo_rows(acc_in, low_ref, high_ref, weight_ref, acc_ref, wide):
@@ -192,7 +188,7 @@
     return 0.5 * x * (1.0 + lax.erf(x * (0.5**0.5)))
 
 
-def block_of(conv_rows, inputs, lines_ref, expand_ref, shrink_ref, normed, hidden):
+def block_of(conv_rows, inputs, lines_ref, expand_ref, shrink_ref, normed, hidden, copies=()):
     gain, norm_bias, shrink_bias, scale = (lines_ref[k : k + 1, :] for k in range(4))
     for i in range(CELLS_R):
         conv = conv_rows(i)
@@ -206,6 +202,8 @@
         lanes = slice(k * WIDTH, (k + 1) * WIDTH)
         part = jnp.dot(normed[...], expand_ref[:, lanes], preferred_element_type=jnp.float32)
         hidden[:, lanes] = gelu(part + lines_ref[4 + k : 5 + k, :]).astype(jnp.bfloat16)
+    for copy in copies:
+        copy.wait()
     shrunk = jnp.dot(hidden[...], shrink_ref[...], preferred_element_type=jnp.float32)
     shrunk = shrunk + shrink_bias
     inputs = inputs.reshape(CELLS_R * HALF, WIDTH).astype(jnp.float32)
@@ -230,19 +228,41 @@
     x_ref,
     lines_ref,
     expand_ref,
-    shrink_ref,
+    shrink_hbm,
     key_ref,
     turned_ref,
+    query_ref,
     sides_ref,
     block_ref,
     keys_ref,
     values_ref,
+    shrink_ref,
+    big_ref,
     wide,
     acc_ref,
     normed,
     hidden,
+    sems,
 ):
+    copies = [
+        pltpu.make_async_copy(
+            shrink_hbm.at[k * WIDTH : (k + 1) * WIDTH],
+            shrink_ref.at[k * WIDTH : (k + 1) * WIDTH],
+            sems.at[k],
+        )
+        for k in range(HID // WIDTH)
+    ]
+    for copy in copies:
+        copy.start()
     halo_rows(acc_in, low_ref, high_ref, weight_ref, acc_ref, wide)
+    query = query_ref[...].astype(jnp.float32)
+    query = jnp.concatenate([query, query], axis=0).T
+    head = lax.broadcasted_iota(jnp.int32, (WIDTH, LANES), 0) // (WIDTH // NH)
+    half = lax.broadcasted_iota(jnp.int32, (WIDTH, LANES), 1) // NQ
+    for t in range(NH // 2):
+        big_ref[:, t * LANES : (t + 1) * LANES] = jnp.where(
+            head == 2 * t + half, query, 0.0
+        ).astype(jnp.bfloat16)
     sides_ref[:, 0:8, :] = acc_ref[:, 0:8, :]
     sides_ref[:, 8:16, :] = acc_ref[:, CELLS_C - 8 : CELLS_C, :]
     block = block_of(
@@ -253,6 +273,7 @@
         shrink_ref,
         normed,
         hidden,
+        copies,
     )
     block_ref[...] = block.reshape(CELLS_R, HALF, WIDTH)
     keys_ref[...] = keys_of(block, key_ref)
@@ -446,13 +467,17 @@
     )
 
 
-def exchanged(first, last, axis):
+def swapped(near, far, axis):
     count, odd = lax.axis_size(axis), lax.axis_index(axis) % 2 == 1
     inner = [(i, i ^ 1) for i in range(count)]
     outer = [(i, i + 1 if i % 2 else i - 1) for i in range(1, count - 1)]
-    near = lax.ppermute(jnp.where(odd, first, last), axis, inner)
-    far = lax.ppermute(jnp.where(odd, last, first), axis, outer)
+    near, far = lax.ppermute(near, axis, inner), lax.ppermute(far, axis, outer)
     return jnp.where(odd, near, far), jnp.where(odd, far, near)
+
+
+def exchanged(first, last, axis):
+    odd = lax.axis_index(axis) % 2 == 1
+    return swapped(jnp.where(odd, first, last), jnp.where(odd, last, first), axis)
 
 
 def per_device(
@@ -477,34 +502,46 @@
     f32, bf16 = jnp.float32, jnp.bfloat16
     hbm, whole = pl.BlockSpec(memory_space=pltpu.HBM), pl.BlockSpec(memory_space=pltpu.VMEM)
     shaped = jax.ShapeDtypeStruct
-    low, high = exchanged(features[:3], features[-3:], "row")
-    acc, first, last, cells, taps_, expand, shrink, key, turned, big, lines = call(
+    cells, taps_, bias, near, far, first, last = call(
+        fetch_kernel,
+        (
+            shaped(features.shape, bf16),
+            shaped(depth_weight.shape, f32),
+            shaped(depth_bias.shape, f32),
+            *[shaped((3, cols, width), bf16)] * 2,
+            *[shaped((rows, 3, width), bf16)] * 2,
+        ),
+        "fetch_cells",
+        *(
+            pltpu.with_memory_space_constraint(array, pltpu.HBM)
+            for array in (features, depth_weight, depth_bias)
+        ),
+        in_specs=[hbm] * 3,
+        out_specs=(whole,) * 7,
+        scratch_shapes=[pltpu.SemaphoreType.DMA((3,))],
+    )
+    low, high = swapped(near, far, "row")
+    acc, expand, key, turned, query, lines = call(
         own_kernel,
         (
             shaped((rows, cols, width), f32),
-            shaped((rows, 3, width), bf16),
-            shaped((rows, 3, width), bf16),
-            shaped(features.shape, bf16),
-            shaped(depth_weight.shape, f32),
             shaped(expand_weight.shape, bf16),
-            shaped(shrink_weight.shape, bf16),
             shaped(key_weight.shape, bf16),
             shaped(value_weight.shape, bf16),
-            shaped((width, NH * NQ), bf16),
+            shaped(queries.shape, bf16),
             shaped((16, width), f32),
         ),
         "own_cells",
+        cells,
+        taps_,
+        bias,
         *(
             pltpu.with_memory_space_constraint(array, pltpu.HBM)
             for array in (
-                features,
-                depth_weight,
                 expand_weight,
-                shrink_weight,
                 key_weight,
                 value_weight,
                 queries,
-                depth_bias,
                 norm_gain,
                 norm_bias,
                 shrink_bias,
@@ -512,17 +549,17 @@
                 expand_bias,
             )
         ),
-        in_specs=[hbm] * 13,
-        out_specs=(whole,) * 11,
+        in_specs=[whole] * 3 + [hbm] * 9,
+        out_specs=(whole,) * 6,
         scratch_shapes=[
             vmem(3, rows, cols + 16, LANES),
             pltpu.VMEM(value_weight.shape, bf16),
-            pltpu.VMEM(queries.shape, bf16),
-            *(vmem(width) for _ in range(5)),
+            *(vmem(width) for _ in range(4)),
             vmem(HID),
-            pltpu.SemaphoreType.DMA((13,)),
+            pltpu.SemaphoreType.DMA((11,)),
         ],
     )
+    first, last, acc = lax.optimization_barrier((first, last, acc))
     left, right = exchanged(
         jnp.concatenate([low[:, :3], first, high[:, :3]], axis=0),
         jnp.concatenate([low[:, -3:], last, high[:, -3:]], axis=0),
@@ -530,13 +567,15 @@
     )
     count = rows * HALF
     work = [pltpu.VMEM((count, width), bf16), pltpu.VMEM((count, HID), bf16)]
-    sides, inner, keys, values = call(
+    sides, inner, keys, values, shrink, big = call(
         inner_kernel,
         (
             shaped((rows, HALF, width), f32),
             shaped((rows, HALF, width), bf16),
             shaped((count, width), bf16),
             shaped((width, count), bf16),
+            shaped(shrink_weight.shape, bf16),
+            shaped((width, NH * NQ), bf16),
         ),
         "inner_cells",
         acc,
@@ -546,10 +585,18 @@
         cells,
         lines,
         expand,
-        shrink,
+        pltpu.with_memory_space_constraint(shrink_weight, pltpu.HBM),
         key,
         turned,
-        scratch_shapes=[vmem(3, 6, cols + 16, LANES), vmem(rows, cols, width), *work],
+        query,
+        in_specs=[whole] * 7 + [hbm] + [whole] * 3,
+        out_specs=(whole,) * 6,
+        scratch_shapes=[
+            vmem(3, 6, cols + 16, LANES),
+            vmem(rows, cols, width),
+            *work,
+            pltpu.SemaphoreType.DMA((HID // width,)),
+        ],
     )
     block_out, part = call(
         outer_kernel,

time: 73.1 us -> 72.4 us (level)
  other arithmetic: 1.08 us -> 0.14 us
    select_n x4 -> x3, other arithmetic: 1.08 us -> 0.14 us  [the longest x1 0.07 us: exchanged(): jnp.where(odd, last, first)]
    pallas_call x6 -> x7, Pallas kernels: 8.89 us -> 9.61 us  [call(): pl.pallas_call(kernel, out_shape=out_shape, name=name, **more, **params())]
  transfers between devices with their start and end apart: 4 -> 4, of which waited for: 1 -> 1; matrix products, arithmetic and copies ran while one was open for 0% -> 0% of each run, Pallas kernels for 6% -> 5%
where the time goes in v3:
time: 72.4 us; the launch traced here: 72 us
  blocking collectives  48.5 us (67%)
  starting transfers between devices  12.8 us (18%)
  Pallas kernels  9.61 us (13%)
  between operations  0.81 us (1%)
    all_to_all x3, blocking collectives, everyone(): lax.all_to_all(part, ('row', 'col'), 0, 0, axis_index_groups=groups, tile...  48.5 us
    pallas_call x7, Pallas kernels, call(): pl.pallas_call(kernel, out_shape=out_shape, name=name, **more, **params())  9.61 us
    ppermute x2, starting transfers between devices, swapped(): lax.ppermute(near, axis, inner)  7.67 us
    ppermute x2, starting transfers between devices, swapped(): lax.ppermute(far, axis, outer)  5.17 us
  transfers between devices with their start and end apart: 4, of which 1 were waited for; matrix products, arithmetic and copies ran while one was open for 0% of the time, Pallas kernels for 5%

profile of v3, /device:TPU:1, one launch (start us, length us, event | category | flops | bytes accessed | tf_op | source)
XLA Modules:
  0.0 72.0 jit_solution(1474805513395503555)
XLA Ops:
  0.6 1.0 %fetch_cells.1 = (bf16[8,32,384]{2,1,0:T(8,128)(2,1)S(1)}, f32[7,7,384]{2,1,0:T(8,128)S(1)}, f32[384]{0:T(512)S(1)}, bf16[3,32,384]{2,1,0:T(8,128)(2,1)S(1)}, bf...) custom-call(bf16[8,32,384]{2,1,0:T(8,128)(2,1)} %x_hbm.1, ...), custom_call_target="tpu_custom_call" | custom-call | flops 1000000 | bytes 1000000 | tf_op jit(solution)/shard_map/fetch_cells/pallas_call | solution.py:439
  1.7 4.5 %collective-permute-start.1 = (bf16[3,32,384]{2,1,0:T(8,128)(2,1)S(1)}, bf16[3,32,384]{2,1,0:T(8,128)(2,1)S(1)}, u32[]{:S(2)}, u32[]{:S(2)}) collective-permute-start(bf16[3,32,384]{2,1,0:T(8,128)(2,1)S(1)} %get-tuple-element.37), channel_id=1, source_target_pairs={{8,16},{16,8},{24,32},{32,24},{40,48},{48,40},{56,64},{64,56},{72,... | collective-permute-start | bytes 221192 | tf_op jit(solution)/shard_map/ppermute | solution.py:474
  6.2 4.9 %collective-permute-start = (bf16[3,32,384]{2,1,0:T(8,128)(2,1)S(1)}, bf16[3,32,384]{2,1,0:T(8,128)(2,1)S(1)}, u32[]{:S(2)}, u32[]{:S(2)}) collective-permute-start(bf16[3,32,384]{2,1,0:T(8,128)(2,1)S(1)} %get-tuple-element.36), channel_id=1, source_target_pairs={{0,8},{8,0},{16,24},{24,16},{32,40},{40,32},{48,56},{56,48},{64,72... | collective-permute-start | bytes 221192 | tf_op jit(solution)/shard_map/ppermute | solution.py:474
  11.1 1.8 %own_cells.1 = (f32[8,32,384]{2,1,0:T(8,128)S(1)}, bf16[384,1536]{1,0:T(8,128)(2,1)S(1)}, bf16[384,384]{1,0:T(8,128)(2,1)S(1)}, bf16[384,384]{1,0:T(8,128)(2,1)S...) custom-call(bf16[8,32,384]{2,1,0:T(8,128)(2,1)S(1)} %get-tuple-element.31.x_ref, ...), custom_call_target="tpu_custom_call" | custom-call | flops 1000000 | bytes 1000000 | tf_op jit(solution)/shard_map/own_cells/pallas_call | solution.py:439
  13.0 0.0 collective-permute-done.1
  13.0 0.0 collective-permute-done
  13.0 0.1 broadcast_select_fusion.4
  13.1 0.7 collective-permute-start.3
  13.8 2.7 %collective-permute-start.2 = (bf16[14,3,384]{2,1,0:T(4,128)(2,1)S(1)}, bf16[14,3,384]{2,1,0:T(4,128)(2,1)S(1)}, u32[]{:S(2)}, u32[]{:S(2)}) collective-permute-start(bf16[14,3,384]{2,1,0:T(4,128)(2,1)S(1)} %get-tuple-element.60), channel_id=1, source_target_pairs={{0,1},{1,0},{2,3},{3,2},{4,5},{5,4},{6,7},{7,6},{8,9},{9,8},{10,11... | collective-permute-start | bytes 96776 | tf_op jit(solution)/shard_map/ppermute | solution.py:474
  16.5 0.0 copy-start.1
  16.5 1.9 %inner_cells.1 = (f32[8,16,384]{2,1,0:T(8,128)S(1)}, bf16[8,16,384]{2,1,0:T(8,128)(2,1)S(1)}, bf16[128,384]{1,0:T(8,128)(2,1)S(1)}, bf16[384,128]{1,0:T(8,128)(2...) custom-call(f32[8,32,384]{2,1,0:T(8,128)S(1)} %get-tuple-element.35.acc_in, ...), custom_call_target="tpu_custom_call" | custom-call | flops 1000000 | bytes 1000000 | tf_op jit(solution)/shard_map/inner_cells/pallas_call | solution.py:439
  18.5 0.0 collective-permute-done.3
  18.5 0.1 collective-permute-done.2
  18.6 0.0 copy-done.1
  18.6 3.1 %outer_cells.1 = (bf16[8,32,384]{2,1,0:T(8,128)(2,1)}, bf16[2,64,512]{2,1,0:T(8,128)(2,1)S(1)}) custom-call(s32[1,4]{1,0:T(1,128)S(1)} %copy-done.1, f32[8,16,384]{2,1,0:T(8,128)S(1)} %get-tuple-element.43.acc_in, bf16[14,3,384]{2,1,0:T(4,128)(2,1)S(1)} %get-tuple-element.58.left_ref, bf16[14,3,384]{2,1,0:T(4,128)(2,1)S(1)} %get-tuple-element.57.right_ref, ...), custom_call_target="tpu_custom_call" | custom-call | flops 1000000 | bytes 1000000 | tf_op jit(solution)/shard_map/outer_cells/pallas_call | solution.py:439
  21.7 0.0 copy-start
  21.7 0.0 copy-start.2
  21.8 13.6 %all_to_all.15.parts_ref = bf16[16,8,512]{2,1,0:T(8,128)(2,1)S(1)} all-to-all(bf16[16,8,512]{2,1,0:T(8,128)(2,1)S(1)} %bitcast.2), channel_id=1, replica_groups={{0,8,16,24,32,40,48,56,64,72,80,88,96,104,112,120},{1,9,17,25,33,41,49,..., dimensions={0} | all-to-all | bytes 262144 | tf_op jit(solution)/shard_map/all_to_all | solution.py:435
  35.4 0.3 merge_first.1
  35.6 24.1 %all_to_all.16.parts_ref = bf16[16,8,512]{2,1,0:T(8,128)(2,1)S(1)} all-to-all(bf16[16,8,512]{2,1,0:T(8,128)(2,1)S(1)} %merge_first.1), channel_id=1, replica_groups={{0,2,4,6,128,130,132,134,256,258,260,262,384,386,388,390},{1,3,5,7,129,..., dimensions={0} | all-to-all | bytes 262144 | tf_op jit(solution)/shard_map/all_to_all | solution.py:435
  59.8 0.3 merge_second.1
  60.1 10.8 %all_to_all.17.parts_ref = bf16[16,8,512]{2,1,0:T(8,128)(2,1)S(1)} all-to-all(bf16[16,8,512]{2,1,0:T(8,128)(2,1)S(1)} %merge_second.1), channel_id=1, replica_groups={{0,8,16,24,32,40,48,56,1,9,17,25,33,41,49,57},{2,10,18,26,34,42,50,58,3..., dimensions={0} | all-to-all | bytes 262144 | tf_op jit(solution)/shard_map/all_to_all | solution.py:435
  70.8 0.0 copy-done
  70.8 0.0 copy-done.2
  70.8 1.2 %pool.1 = (f32[64,384]{1,0:T(8,128)}, f32[1]{0:T(128)}) custom-call(bf16[16,8,512]{2,1,0:T(8,128)(2,1)S(1)} %all_to_all.17.parts_ref, f32[16,384]{1,0:T(8,128)S(1)} %bitcast.3, s32[16]{0:T(128)S(1)} %copy-done.2), custom_call_target="tpu_custom_call" | custom-call | flops 1000000 | bytes 1000000 | tf_op jit(solution)/shard_map/pool/pallas_call | solution.py:439
  (3 shorter events, 0.1 us)
Async XLA Ops:
  1.7 11.3 %collective-permute-start.1 = (bf16[3,32,384]{2,1,0:T(8,128)(2,1)S(1)}, bf16[3,32,384]{2,1,0:T(8,128)(2,1)S(1)}, u32[]{:S(2)}, u32[]{:S(2)}) collective-permute-start(bf16[3,32,384]{2,1,0:T(8,128)(2,1)S(1)} %get-tuple-element.37), channel_id=1, source_target_pairs={{8,16},{16,8},{24,32},{32,24},{40,48},{48,40},{56,64},{64,56},{72,... | collective-permute-start | bytes 221192 | tf_op jit(solution)/shard_map/ppermute | solution.py:474
  6.2 6.8 %collective-permute-start = (bf16[3,32,384]{2,1,0:T(8,128)(2,1)S(1)}, bf16[3,32,384]{2,1,0:T(8,128)(2,1)S(1)}, u32[]{:S(2)}, u32[]{:S(2)}) collective-permute-start(bf16[3,32,384]{2,1,0:T(8,128)(2,1)S(1)} %get-tuple-element.36), channel_id=1, source_target_pairs={{0,8},{8,0},{16,24},{24,16},{32,40},{40,32},{48,56},{56,48},{64,72... | collective-permute-start | bytes 221192 | tf_op jit(solution)/shard_map/ppermute | solution.py:474
  13.1 5.4 %collective-permute-start.3 = (bf16[14,3,384]{2,1,0:T(4,128)(2,1)S(1)}, bf16[14,3,384]{2,1,0:T(4,128)(2,1)S(1)}, u32[]{:S(2)}, u32[]{:S(2)}) collective-permute-start(bf16[14,3,384]{2,1,0:T(4,128)(2,1)S(1)} %get-tuple-element.59), channel_id=1, source_target_pairs={{1,2},{2,1},{3,4},{4,3},{5,6},{6,5},{9,10},{10,9},{11,12},{12,11},... | collective-permute-start | bytes 96776 | tf_op jit(solution)/shard_map/ppermute | solution.py:474
  13.8 4.8 %collective-permute-start.2 = (bf16[14,3,384]{2,1,0:T(4,128)(2,1)S(1)}, bf16[14,3,384]{2,1,0:T(4,128)(2,1)S(1)}, u32[]{:S(2)}, u32[]{:S(2)}) collective-permute-start(bf16[14,3,384]{2,1,0:T(4,128)(2,1)S(1)} %get-tuple-element.60), channel_id=1, source_target_pairs={{0,1},{1,0},{2,3},{3,2},{4,5},{5,4},{6,7},{7,6},{8,9},{9,8},{10,11... | collective-permute-start | bytes 96776 | tf_op jit(solution)/shard_map/ppermute | solution.py:474
  16.5 2.1 %copy-start.1 = (s32[1,4]{1,0:T(1,128)S(1)}, s32[1,4]{1,0:T(1,128)}, u32[]{:S(2)}) copy-start(s32[1,4]{1,0:T(1,128)} %tissue_ref.1) | copy-start | bytes 52
  21.7 49.1 %copy-start = (f32[384,16]{0,1:T(8,128)S(1)}, f32[384,16]{0,1:T(8,128)}, u32[]{:S(2)}) copy-start(f32[384,16]{0,1:T(8,128)} %param.29) | copy-start | bytes 73732
  21.7 49.1 %copy-start.2 = (s32[16]{0:T(128)S(1)}, s32[16]{0:T(128)}, u32[]{:S(2)}) copy-start(s32[16]{0:T(128)} %label_ref.1) | copy-start | bytes 196

commit v4 on v3

--- a/solution.py
+++ b/solution.py
@@ -16,22 +16,16 @@
 
 
 EIGHT, FOUR, TWO = range(8), range(4), range(2)
-FIRST = [[device(2 * z + k, n, y) for k in TWO for n in EIGHT] for z in FOUR for y in EIGHT]
-SECOND = [
-    [device(2 * z + k, n, 2 * y + m) for z in FOUR for y in FOUR]
-    for k in TWO
-    for n in EIGHT
-    for m in TWO
-]
-THIRD = [[device(z, n, 2 * y + m) for m in TWO for n in EIGHT] for z in EIGHT for y in FOUR]
-
-
+SHARES = [[device(2 * z + k, n, y) for k in TWO for n in EIGHT] for z in FOUR for y in EIGHT]
+REST = [[device(2 * z + k, n, y) for z in FOUR for y in EIGHT] for k in TWO for n in EIGHT]
 WIDTH = 384
 LANES = 128
 CELLS_R = 8
 CELLS_C = 32
 HID = 1536
 HALF = 16
+SHARE = 192
+MARK = SHARE - LANES
 
 
 def taps(acc, rows, weight_ref, lanes, b, first):
@@ -286,7 +280,9 @@
     middle = rest.astype(jnp.bfloat16).astype(jnp.float32)
     low = (rest - middle).astype(jnp.bfloat16).astype(jnp.float32)
     marks = high + pltpu.roll(middle, NH, 1) + pltpu.roll(low, 2 * NH, 1)
-    return jnp.concatenate([weighted, marks], axis=1).astype(jnp.bfloat16)
+    lane = lax.broadcasted_iota(jnp.int32, marks.shape, 1)
+    last = jnp.where(lane < MARK, weighted[:, LANES:], marks)
+    return jnp.concatenate([weighted[:, :LANES], last], axis=1).astype(jnp.bfloat16)
 
 
 def outer_kernel(
@@ -340,82 +336,91 @@
     line = lax.broadcasted_iota(jnp.int32, (NH, LANES), 0)
     tops = jnp.zeros((NH, LANES), jnp.float32)
     totals = jnp.zeros((NH, LANES), jnp.float32)
+    scores = jnp.dot(keys, big_ref[...], preferred_element_type=jnp.float32)
+    scores = (scores * (size**-0.5 * LOG2E)).reshape(2, CELLS_R, 2, TILE, NH * NQ)
+    scores = [[jnp.where(live[h][g], scores[h, :, g], -1e30) for g in range(2)] for h in range(2)]
+    all_top = jnp.maximum(
+        jnp.maximum(scores[0][0], scores[0][1]), jnp.maximum(scores[1][0], scores[1][1])
+    )
+    all_top = jnp.ceil(jnp.max(jnp.max(all_top, axis=0), axis=0, keepdims=True))
+    weights = [
+        [jnp.where(live[h][g], jnp.exp2(scores[h][g] - all_top), 0.0) for g in range(2)]
+        for h in range(2)
+    ]
+    all_total = (weights[0][0] + weights[0][1]) + (weights[1][0] + weights[1][1])
+    all_total = jnp.sum(jnp.sum(all_total, axis=0), axis=0, keepdims=True)
+    weights = [jnp.stack(pair, axis=1).reshape(CELLS_R * HALF, NH * NQ) for pair in weights]
+    weights = jnp.concatenate(weights, axis=0).astype(jnp.bfloat16)
     for t in range(NH // 2):
-        scores = jnp.dot(
-            keys, big_ref[:, t * LANES : (t + 1) * LANES], preferred_element_type=jnp.float32
-        ) * (size**-0.5 * LOG2E)
-        scores = scores.reshape(2, CELLS_R, 2, TILE, LANES)
-        scores = [
-            [jnp.where(live[h][g], scores[h, :, g], -1e30) for g in range(2)] for h in range(2)
-        ]
-        top = jnp.maximum(
-            jnp.maximum(scores[0][0], scores[0][1]), jnp.maximum(scores[1][0], scores[1][1])
+        lanes = slice(t * LANES, (t + 1) * LANES)
+        top, total = all_top[:, lanes], all_total[:, lanes]
+        pair = jnp.dot(
+            values[2 * size * t : 2 * size * (t + 1), :],
+            weights[:, lanes],
+            preferred_element_type=jnp.float32,
         )
-        top = jnp.ceil(jnp.max(jnp.max(top, axis=0), axis=0, keepdims=True))
-        weights = [
-            [jnp.where(live[h][g], jnp.exp2(scores[h][g] - top), 0.0) for g in range(2)]
-            for h in range(2)
-        ]
-        total = (weights[0][0] + weights[0][1]) + (weights[1][0] + weights[1][1])
-        total = jnp.sum(jnp.sum(total, axis=0), axis=0, keepdims=True)
-        weights = [jnp.stack(pair, axis=1).reshape(CELLS_R * HALF, LANES) for pair in weights]
-        weights = jnp.concatenate(weights, axis=0).astype(jnp.bfloat16)
-        pair = jnp.dot(
-            values[2 * size * t : 2 * size * (t + 1), :], weights, preferred_element_type=jnp.float32
-        )
-        sums[2 * size * t : 2 * size * t + size, :] = pair[:size]
-        sums[2 * size * t + size : 2 * size * (t + 1), :] = pltpu.roll(pair[size:], NQ, 1)
+        at = 2 * size * t + (t // 2) * (256 - SHARE)
+        sums[at : at + size, :] = pair[:size]
+        sums[at + size : at + 2 * size, :] = pltpu.roll(pair[size:], NQ, 1)
         top = jnp.broadcast_to(top, (NH, LANES))
         total = jnp.broadcast_to(total, (NH, LANES))
         tops = jnp.where(line == 2 * t, top, tops)
         tops = jnp.where(line == 2 * t + 1, pltpu.roll(top, NQ, 1), tops)
         totals = jnp.where(line == 2 * t, total, totals)
         totals = jnp.where(line == 2 * t + 1, pltpu.roll(total, NQ, 1), totals)
-    sums[WIDTH:, :] = jnp.zeros((LANES, LANES), jnp.float32)
-    sums[WIDTH : WIDTH + NH, :] = tops
-    sums[WIDTH + 3 * NH : WIDTH + 4 * NH, :] = totals
+    for u in range(2):
+        at = 256 * u + SHARE
+        sums[at : at + 64, :] = jnp.zeros((64, LANES), jnp.float32)
+        sums[at : at + NH, :] = pltpu.roll(tops, 4, 0) if u else tops
+        sums[at + 3 * NH : at + 4 * NH, :] = pltpu.roll(totals, 4, 0) if u else totals
     part = sums[...].T
-    part_ref[...] = jnp.broadcast_to(
-        marked(part[:NQ, :WIDTH], part[:NQ, WIDTH:])[None], part_ref.shape
-    )
+    for u in range(2):
+        share = part[:NQ, 256 * u : 256 * (u + 1)]
+        lane = lax.broadcasted_iota(jnp.int32, (NQ, LANES), 1)
+        part_ref[u] = marked(share, jnp.where(lane < MARK, 0.0, share[:, LANES:]))
     copy.wait()
 
 
 def spread_matrix(first, copies):
-    lane = lax.broadcasted_iota(jnp.int32, (LANES, WIDTH), 0) - first
-    head = lax.broadcasted_iota(jnp.int32, (LANES, WIDTH), 1) // (WIDTH // NH)
-    inside = (lane >= 0) & (lane < copies * NH)
+    lane = lax.broadcasted_iota(jnp.int32, (LANES, 256), 0) - first
+    head = lax.broadcasted_iota(jnp.int32, (LANES, 256), 1) // (WIDTH // NH)
+    inside = (lane >= 0) & (lane < copies * NH) & (head < 4)
     return jnp.where(inside & (lane % NH == head), 1.0, 0.0).astype(jnp.bfloat16)
 
 
-def combined(parts):
-    n, q = parts.shape[:2]
-    parts = parts.astype(jnp.float32)
-    marks = parts[:, :, WIDTH:].reshape(n * q, LANES)
+def merge_kernel(parts_ref, out_ref):
+    n, q, width = parts_ref.shape
+    parts = parts_ref[...].astype(jnp.float32)
+    lane = lax.broadcasted_iota(jnp.int32, (n * q, LANES), 1)
+    marks = parts[:, :, LANES:].reshape(n * q, LANES)
+    marks = jnp.where(lane < MARK, 0.0, marks)
     marks = marks + pltpu.roll(marks, LANES - NH, 1) + pltpu.roll(marks, LANES - 2 * NH, 1)
     top = jnp.max(marks.reshape(n, q, LANES), axis=0)
     factor = jnp.exp2(marks.reshape(n, q, LANES) - top).reshape(n * q, LANES)
     factor = factor.astype(jnp.bfloat16)
-    spread = jnp.dot(factor, spread_matrix(0, 1), preferred_element_type=jnp.float32)
-    weighted = jnp.sum(parts[:, :, :WIDTH] * spread.reshape(n, q, WIDTH), axis=0)
+    spread = jnp.dot(factor, spread_matrix(MARK, 1), preferred_element_type=jnp.float32)
+    weighted = jnp.sum(parts * spread.reshape(n, q, width), axis=0)
     total = marks * pltpu.roll(factor.astype(jnp.float32), 3 * NH, 1)
     total = jnp.sum(total.reshape(n, q, LANES), axis=0)
-    lane = lax.broadcasted_iota(jnp.int32, (q, LANES), 1)
-    inside = (lane >= 3 * NH) & (lane < 4 * NH)
-    return weighted, jnp.where(lane < NH, top, 0.0), jnp.where(inside, total, 1.0), inside
-
-
-def merge_kernel(parts_ref, out_ref):
-    weighted, top, total, inside = combined(parts_ref[...])
-    part = marked(weighted, top + jnp.where(inside, total, 0.0))
-    out_ref[...] = jnp.broadcast_to(part[None], out_ref.shape)
+    lane = lane[:q]
+    part = jnp.where((lane >= MARK) & (lane < MARK + 4), top, 0.0)
+    part = jnp.where((lane >= MARK + 3 * NH) & (lane < MARK + 3 * NH + 4), total, part)
+    share = marked(weighted, part)
+    out_ref[...] = jnp.broadcast_to(share[None], out_ref.shape)
 
 
 def pool_kernel(parts_ref, class_ref, label_ref, out_ref, loss_ref):
-    weighted, _, total, inside = combined(parts_ref[...].reshape(2, NQ, WIDTH + LANES))
-    marks = marked(weighted, jnp.where(inside, 1.0 / total, 0.0))[:, WIDTH:]
-    inverse = jnp.dot(marks, spread_matrix(3 * NH, 3), preferred_element_type=jnp.float32)
-    pooled = weighted * inverse
+    parts = parts_ref[...].reshape(2 * NQ, 256).astype(jnp.float32)
+    lane = lax.broadcasted_iota(jnp.int32, (2 * NQ, LANES), 1)
+    first = MARK + 3 * NH
+    marks = jnp.where(lane < MARK, 0.0, parts[:, LANES:])
+    marks = marks + pltpu.roll(marks, LANES - NH, 1) + pltpu.roll(marks, LANES - 2 * NH, 1)
+    inside = (lane >= first) & (lane < first + 4)
+    marks = jnp.where(inside, 1.0 / jnp.where(inside, marks, 1.0), 0.0)
+    marks = marked(parts, marks)[:, LANES:]
+    inverse = jnp.dot(marks, spread_matrix(first, 3), preferred_element_type=jnp.float32)
+    pooled = (parts * inverse).reshape(2, NQ, 256)
+    pooled = jnp.concatenate([pooled[0, :, :SHARE], pooled[1, :, :SHARE]], axis=1)
     out_ref[...] = pooled
     lines = jnp.sum(pooled.reshape(NQ // 8, 8, WIDTH), axis=0)
     logits = lax.dot_general(
@@ -440,11 +445,10 @@
 
 
 def merged(part, class_weight, slide_label):
-    chunk = (16, NQ // 8, WIDTH + LANES)
-    same = jax.ShapeDtypeStruct(chunk, jnp.bfloat16)
-    parts = everyone(part.reshape(chunk), FIRST)
-    parts = everyone(call(merge_kernel, same, "merge_first", parts), SECOND)
-    parts = everyone(call(merge_kernel, same, "merge_second", parts), THIRD)
+    rest, shares = (jax.ShapeDtypeStruct((n, NQ // 8, 256), jnp.bfloat16) for n in (32, 16))
+    parts = everyone(part.reshape(shares.shape), SHARES)
+    parts = everyone(call(merge_kernel, rest, "merge_first", parts), REST)
+    parts = everyone(call(merge_kernel, shares, "merge_second", parts), SHARES)
     return call(
         pool_kernel,
         (jax.ShapeDtypeStruct((NQ, WIDTH), jnp.float32), jax.ShapeDtypeStruct((1,), jnp.float32)),
@@ -600,7 +604,7 @@
     )
     block_out, part = call(
         outer_kernel,
-        (shaped((rows, cols, width), bf16), shaped((2, NQ, width + LANES), bf16)),
+        (shaped((rows, cols, width), bf16), shaped((2, NQ, 256), bf16)),
         "outer_cells",
         tissue,
         sides,

time: 72.4 us -> 71.9 us (level)
  no operation moved by 1% of the time
where the time goes in v4:
time: 71.9 us; the launch traced here: 71.5 us
  blocking collectives  48.4 us (67%)
  starting transfers between devices  12.8 us (18%)
  Pallas kernels  9.18 us (13%)
  between operations  0.81 us (1%)
    all_to_all x3, blocking collectives, everyone(): lax.all_to_all(part, ('row', 'col'), 0, 0, axis_index_groups=groups, tile...  48.4 us
    pallas_call x7, Pallas kernels, call(): pl.pallas_call(kernel, out_shape=out_shape, name=name, **more, **params())  9.18 us
    ppermute x2, starting transfers between devices, swapped(): lax.ppermute(near, axis, inner)  7.67 us
    ppermute x2, starting transfers between devices, swapped(): lax.ppermute(far, axis, outer)  5.17 us
  transfers between devices with their start and end apart: 4, of which 1 were waited for; matrix products, arithmetic and copies ran while one was open for 0% of the time, Pallas kernels for 5%

profile of v4, /device:TPU:1, one launch (start us, length us, event | category | flops | bytes accessed | tf_op | source)
XLA Modules:
  0.0 71.5 jit_solution(5325966827189933337)
XLA Ops:
  0.6 1.0 %fetch_cells.1 = (bf16[8,32,384]{2,1,0:T(8,128)(2,1)S(1)}, f32[7,7,384]{2,1,0:T(8,128)S(1)}, f32[384]{0:T(512)S(1)}, bf16[3,32,384]{2,1,0:T(8,128)(2,1)S(1)}, bf...) custom-call(bf16[8,32,384]{2,1,0:T(8,128)(2,1)} %x_hbm.1, ...), custom_call_target="tpu_custom_call" | custom-call | flops 1000000 | bytes 1000000 | tf_op jit(solution)/shard_map/fetch_cells/pallas_call | solution.py:444
  1.7 4.5 %collective-permute-start.1 = (bf16[3,32,384]{2,1,0:T(8,128)(2,1)S(1)}, bf16[3,32,384]{2,1,0:T(8,128)(2,1)S(1)}, u32[]{:S(2)}, u32[]{:S(2)}) collective-permute-start(bf16[3,32,384]{2,1,0:T(8,128)(2,1)S(1)} %get-tuple-element.37), channel_id=1, source_target_pairs={{8,16},{16,8},{24,32},{32,24},{40,48},{48,40},{56,64},{64,56},{72,... | collective-permute-start | bytes 221192 | tf_op jit(solution)/shard_map/ppermute | solution.py:478
  6.2 4.9 %collective-permute-start = (bf16[3,32,384]{2,1,0:T(8,128)(2,1)S(1)}, bf16[3,32,384]{2,1,0:T(8,128)(2,1)S(1)}, u32[]{:S(2)}, u32[]{:S(2)}) collective-permute-start(bf16[3,32,384]{2,1,0:T(8,128)(2,1)S(1)} %get-tuple-element.36), channel_id=1, source_target_pairs={{0,8},{8,0},{16,24},{24,16},{32,40},{40,32},{48,56},{56,48},{64,72... | collective-permute-start | bytes 221192 | tf_op jit(solution)/shard_map/ppermute | solution.py:478
  11.1 1.8 %own_cells.1 = (f32[8,32,384]{2,1,0:T(8,128)S(1)}, bf16[384,1536]{1,0:T(8,128)(2,1)S(1)}, bf16[384,384]{1,0:T(8,128)(2,1)S(1)}, bf16[384,384]{1,0:T(8,128)(2,1)S...) custom-call(bf16[8,32,384]{2,1,0:T(8,128)(2,1)S(1)} %get-tuple-element.31.x_ref, ...), custom_call_target="tpu_custom_call" | custom-call | flops 1000000 | bytes 1000000 | tf_op jit(solution)/shard_map/own_cells/pallas_call | solution.py:444
  13.0 0.0 collective-permute-done.1
  13.0 0.0 collective-permute-done
  13.0 0.1 broadcast_select_fusion.4
  13.1 0.7 collective-permute-start.3
  13.8 2.7 %collective-permute-start.2 = (bf16[14,3,384]{2,1,0:T(4,128)(2,1)S(1)}, bf16[14,3,384]{2,1,0:T(4,128)(2,1)S(1)}, u32[]{:S(2)}, u32[]{:S(2)}) collective-permute-start(bf16[14,3,384]{2,1,0:T(4,128)(2,1)S(1)} %get-tuple-element.60), channel_id=1, source_target_pairs={{0,1},{1,0},{2,3},{3,2},{4,5},{5,4},{6,7},{7,6},{8,9},{9,8},{10,11... | collective-permute-start | bytes 96776 | tf_op jit(solution)/shard_map/ppermute | solution.py:478
  16.5 0.0 copy-start.1
  16.5 1.9 %inner_cells.1 = (f32[8,16,384]{2,1,0:T(8,128)S(1)}, bf16[8,16,384]{2,1,0:T(8,128)(2,1)S(1)}, bf16[128,384]{1,0:T(8,128)(2,1)S(1)}, bf16[384,128]{1,0:T(8,128)(2...) custom-call(f32[8,32,384]{2,1,0:T(8,128)S(1)} %get-tuple-element.35.acc_in, ...), custom_call_target="tpu_custom_call" | custom-call | flops 1000000 | bytes 1000000 | tf_op jit(solution)/shard_map/inner_cells/pallas_call | solution.py:444
  18.5 0.0 collective-permute-done.3
  18.5 0.1 collective-permute-done.2
  18.6 0.0 copy-done.1
  18.6 0.0 copy-start
  18.6 0.0 copy-start.2
  18.6 2.6 %outer_cells.1 = (bf16[8,32,384]{2,1,0:T(8,128)(2,1)}, bf16[2,64,256]{2,1,0:T(8,128)(2,1)S(1)}) custom-call(s32[1,4]{1,0:T(1,128)S(1)} %copy-done.1, f32[8,16,384]{2,1,0:T(8,128)S(1)} %get-tuple-element.43.acc_in, bf16[14,3,384]{2,1,0:T(4,128)(2,1)S(1)} %get-tuple-element.58.left_ref, bf16[14,3,384]{2,1,0:T(4,128)(2,1)S(1)} %get-tuple-element.57.right_ref, ...), custom_call_target="tpu_custom_call" | custom-call | flops 1000000 | bytes 1000000 | tf_op jit(solution)/shard_map/outer_cells/pallas_call | solution.py:444
  21.3 13.3 %all_to_all.15.parts_ref = bf16[16,8,256]{2,1,0:T(8,128)(2,1)S(1)} all-to-all(bf16[16,8,256]{2,1,0:T(8,128)(2,1)S(1)} %bitcast.2), channel_id=1, replica_groups={{0,8,16,24,32,40,48,56,64,72,80,88,96,104,112,120},{1,9,17,25,33,41,49,..., dimensions={0} | all-to-all | bytes 131072 | tf_op jit(solution)/shard_map/all_to_all | solution.py:440
  34.6 0.3 merge_first.1
  34.9 24.8 %all_to_all.16.parts_ref = bf16[32,8,256]{2,1,0:T(8,128)(2,1)S(1)} all-to-all(bf16[32,8,256]{2,1,0:T(8,128)(2,1)S(1)} %merge_first.1), channel_id=1, replica_groups={{0,1,2,3,4,5,6,7,128,129,130,131,132,133,134,135,256,257,258,259,260,26..., dimensions={0} | all-to-all | bytes 262144 | tf_op jit(solution)/shard_map/all_to_all | solution.py:440
  59.6 0.3 merge_second.1
  59.9 10.4 %all_to_all.17.parts_ref = bf16[16,8,256]{2,1,0:T(8,128)(2,1)S(1)} all-to-all(bf16[16,8,256]{2,1,0:T(8,128)(2,1)S(1)} %merge_second.1), channel_id=1, replica_groups={{0,8,16,24,32,40,48,56,64,72,80,88,96,104,112,120},{1,9,17,25,33,41,49,..., dimensions={0} | all-to-all | bytes 131072 | tf_op jit(solution)/shard_map/all_to_all | solution.py:440
  70.3 0.0 copy-done
  70.3 0.0 copy-done.2
  70.3 1.2 %pool.1 = (f32[64,384]{1,0:T(8,128)}, f32[1]{0:T(128)}) custom-call(bf16[16,8,256]{2,1,0:T(8,128)(2,1)S(1)} %all_to_all.17.parts_ref, f32[16,384]{1,0:T(8,128)S(1)} %bitcast.3, s32[16]{0:T(128)S(1)} %copy-done.2), custom_call_target="tpu_custom_call" | custom-call | flops 1000000 | bytes 1000000 | tf_op jit(solution)/shard_map/pool/pallas_call | solution.py:444
  (3 shorter events, 0.1 us)
Async XLA Ops:
  1.7 11.3 %collective-permute-start.1 = (bf16[3,32,384]{2,1,0:T(8,128)(2,1)S(1)}, bf16[3,32,384]{2,1,0:T(8,128)(2,1)S(1)}, u32[]{:S(2)}, u32[]{:S(2)}) collective-permute-start(bf16[3,32,384]{2,1,0:T(8,128)(2,1)S(1)} %get-tuple-element.37), channel_id=1, source_target_pairs={{8,16},{16,8},{24,32},{32,24},{40,48},{48,40},{56,64},{64,56},{72,... | collective-permute-start | bytes 221192 | tf_op jit(solution)/shard_map/ppermute | solution.py:478
  6.2 6.8 %collective-permute-start = (bf16[3,32,384]{2,1,0:T(8,128)(2,1)S(1)}, bf16[3,32,384]{2,1,0:T(8,128)(2,1)S(1)}, u32[]{:S(2)}, u32[]{:S(2)}) collective-permute-start(bf16[3,32,384]{2,1,0:T(8,128)(2,1)S(1)} %get-tuple-element.36), channel_id=1, source_target_pairs={{0,8},{8,0},{16,24},{24,16},{32,40},{40,32},{48,56},{56,48},{64,72... | collective-permute-start | bytes 221192 | tf_op jit(solution)/shard_map/ppermute | solution.py:478
  13.1 5.4 %collective-permute-start.3 = (bf16[14,3,384]{2,1,0:T(4,128)(2,1)S(1)}, bf16[14,3,384]{2,1,0:T(4,128)(2,1)S(1)}, u32[]{:S(2)}, u32[]{:S(2)}) collective-permute-start(bf16[14,3,384]{2,1,0:T(4,128)(2,1)S(1)} %get-tuple-element.59), channel_id=1, source_target_pairs={{1,2},{2,1},{3,4},{4,3},{5,6},{6,5},{9,10},{10,9},{11,12},{12,11},... | collective-permute-start | bytes 96776 | tf_op jit(solution)/shard_map/ppermute | solution.py:478
  13.8 4.8 %collective-permute-start.2 = (bf16[14,3,384]{2,1,0:T(4,128)(2,1)S(1)}, bf16[14,3,384]{2,1,0:T(4,128)(2,1)S(1)}, u32[]{:S(2)}, u32[]{:S(2)}) collective-permute-start(bf16[14,3,384]{2,1,0:T(4,128)(2,1)S(1)} %get-tuple-element.60), channel_id=1, source_target_pairs={{0,1},{1,0},{2,3},{3,2},{4,5},{5,4},{6,7},{7,6},{8,9},{9,8},{10,11... | collective-permute-start | bytes 96776 | tf_op jit(solution)/shard_map/ppermute | solution.py:478
  16.5 2.1 %copy-start.1 = (s32[1,4]{1,0:T(1,128)S(1)}, s32[1,4]{1,0:T(1,128)}, u32[]{:S(2)}) copy-start(s32[1,4]{1,0:T(1,128)} %tissue_ref.1) | copy-start | bytes 52
  18.6 51.7 %copy-start = (f32[384,16]{0,1:T(8,128)S(1)}, f32[384,16]{0,1:T(8,128)}, u32[]{:S(2)}) copy-start(f32[384,16]{0,1:T(8,128)} %param.29) | copy-start | bytes 73732
  18.6 51.7 %copy-start.2 = (s32[16]{0:T(128)S(1)}, s32[16]{0:T(128)}, u32[]{:S(2)}) copy-start(s32[16]{0:T(128)} %label_ref.1) | copy-start | bytes 196

commit v5 on v4

--- a/solution.py
+++ b/solution.py
@@ -60,8 +60,6 @@
     weight_ref,
     bias_ref,
     expand_hbm,
-    key_hbm,
-    value_hbm,
     query_hbm,
     gain_hbm,
     norm_bias_hbm,
@@ -70,12 +68,9 @@
     expand_bias_hbm,
     acc_ref,
     expand_ref,
-    key_ref,
-    turned_ref,
     query_ref,
     rows_ref,
     wide,
-    value_ref,
     gain_ref,
     norm_bias_ref,
     shrink_bias_ref,
@@ -90,8 +85,6 @@
         (scale_hbm, scale_ref),
         (expand_bias_hbm, expand_bias_ref),
         (query_hbm, query_ref),
-        (value_hbm, value_ref),
-        (key_hbm, key_ref),
         *(
             (expand_hbm.at[k : k + LANES], expand_ref.at[k : k + LANES])
             for k in range(0, WIDTH, LANES)
@@ -101,29 +94,31 @@
     for copy in copies:
         copy.start()
     rows_ref[8:9, :] = bias_ref[...].reshape(1, WIDTH)
+    groups = CELLS_C // 8
     for c in range(3):
-        lanes = pl.ds(c * LANES, LANES)
-        wide[c, :, 0:8, :] = jnp.zeros((CELLS_R, 8, LANES), jnp.float32)
-        wide[c, :, 8 + CELLS_C : 16 + CELLS_C, :] = jnp.zeros((CELLS_R, 8, LANES), jnp.float32)
-        wide[c, :, 8 : 8 + CELLS_C, :] = x_ref[:, :, lanes].astype(jnp.float32)
-
-    def lane_tile(c, carry):
+        cells = x_ref[:, :, pl.ds(c * LANES, LANES)].astype(jnp.float32)
+        for j in range(groups):
+            for k in range(3):
+                at = 8 * (j + k - 1)
+                part = jnp.zeros((CELLS_R, 8, LANES), jnp.float32)
+                if 0 <= at < CELLS_C:
+                    part = cells[:, at : at + 8]
+                wide[groups * c + j, :, 8 * k : 8 * k + 8, :] = part
+
+    def lane_tile(step, carry):
+        c, j = step // groups, step % groups
         lanes = pl.ds(pl.multiple_of(c * LANES, LANES), LANES)
-        bias = jnp.broadcast_to(rows_ref[8:9, lanes], (8, LANES))
-        for j in range(CELLS_C // 8):
-            acc = [bias] * CELLS_R
-            for b in range(7):
-                at = 8 * j + 5 + b
-                rows = [wide[c, r, at : at + 8, :] for r in range(CELLS_R)]
-                acc = taps(acc, rows, weight_ref, lanes, b, 0)
-            for i in range(CELLS_R):
-                acc_ref[i, 8 * j : 8 * j + 8, lanes] = acc[i]
+        acc = [jnp.broadcast_to(rows_ref[8:9, lanes], (8, LANES))] * CELLS_R
+        for b in range(7):
+            rows = [wide[step, r, 5 + b : 13 + b, :] for r in range(CELLS_R)]
+            acc = taps(acc, rows, weight_ref, lanes, b, 0)
+        for i in range(CELLS_R):
+            acc_ref[i, pl.ds(pl.multiple_of(8 * j, 8), 8), lanes] = acc[i]
         return carry
 
-    lax.fori_loop(0, 3, lane_tile, 0)
+    lax.fori_loop(0, 3 * groups, lane_tile, 0)
     for copy in copies:
         copy.wait()
-    turned_ref[...] = value_ref[...].astype(jnp.float32).T.astype(jnp.bfloat16)
     for row, ref in enumerate((gain_ref, norm_bias_ref, shrink_bias_ref, scale_ref)):
         rows_ref[row : row + 1, :] = ref[...].reshape(1, WIDTH)
     for k in range(HID // WIDTH):
@@ -223,19 +218,22 @@
     lines_ref,
     expand_ref,
     shrink_hbm,
-    key_ref,
-    turned_ref,
+    key_hbm,
+    value_hbm,
     query_ref,
     sides_ref,
     block_ref,
     keys_ref,
     values_ref,
     shrink_ref,
+    key_ref,
+    turned_ref,
     big_ref,
     wide,
     acc_ref,
     normed,
     hidden,
+    value_ref,
     sems,
 ):
     copies = [
@@ -246,9 +244,16 @@
         )
         for k in range(HID // WIDTH)
     ]
-    for copy in copies:
+    late = [
+        pltpu.make_async_copy(value_hbm, value_ref, sems.at[4]),
+        pltpu.make_async_copy(key_hbm, key_ref, sems.at[5]),
+    ]
+    for copy in copies + late:
         copy.start()
     halo_rows(acc_in, low_ref, high_ref, weight_ref, acc_ref, wide)
+    for copy in late:
+        copy.wait()
+    turned_ref[...] = value_ref[...].astype(jnp.float32).T.astype(jnp.bfloat16)
     query = query_ref[...].astype(jnp.float32)
     query = jnp.concatenate([query, query], axis=0).T
     head = lax.broadcasted_iota(jnp.int32, (WIDTH, LANES), 0) // (WIDTH // NH)
@@ -525,13 +530,11 @@
         scratch_shapes=[pltpu.SemaphoreType.DMA((3,))],
     )
     low, high = swapped(near, far, "row")
-    acc, expand, key, turned, query, lines = call(
+    acc, expand, query, lines = call(
         own_kernel,
         (
             shaped((rows, cols, width), f32),
             shaped(expand_weight.shape, bf16),
-            shaped(key_weight.shape, bf16),
-            shaped(value_weight.shape, bf16),
             shaped(queries.shape, bf16),
             shaped((16, width), f32),
         ),
@@ -543,8 +546,6 @@
             pltpu.with_memory_space_constraint(array, pltpu.HBM)
             for array in (
                 expand_weight,
-                key_weight,
-                value_weight,
                 queries,
                 norm_gain,
                 norm_bias,
@@ -553,14 +554,13 @@
                 expand_bias,
             )
         ),
-        in_specs=[whole] * 3 + [hbm] * 9,
-        out_specs=(whole,) * 6,
+        in_specs=[whole] * 3 + [hbm] * 7,
+        out_specs=(whole,) * 4,
         scratch_shapes=[
-            vmem(3, rows, cols + 16, LANES),
-            pltpu.VMEM(value_weight.shape, bf16),
+            vmem(3 * cols // 8, rows, 24, LANES),
             *(vmem(width) for _ in range(4)),
             vmem(HID),
-            pltpu.SemaphoreType.DMA((11,)),
+            pltpu.SemaphoreType.DMA((9,)),
         ],
     )
     first, last, acc = lax.optimization_barrier((first, last, acc))
@@ -571,7 +571,7 @@
     )
     count = rows * HALF
     work = [pltpu.VMEM((count, width), bf16), pltpu.VMEM((count, HID), bf16)]
-    sides, inner, keys, values, shrink, big = call(
+    sides, inner, keys, values, shrink, key, turned, big = call(
         inner_kernel,
         (
             shaped((rows, HALF, width), f32),
@@ -579,6 +579,8 @@
             shaped((count, width), bf16),
             shaped((width, count), bf16),
             shaped(shrink_weight.shape, bf16),
+            shaped(key_weight.shape, bf16),
+            shaped(value_weight.shape, bf16),
             shaped((width, NH * NQ), bf16),
         ),
         "inner_cells",
@@ -589,17 +591,19 @@
         cells,
         lines,
         expand,
-        pltpu.with_memory_space_constraint(shrink_weight, pltpu.HBM),
-        key,
-        turned,
+        *(
+            pltpu.with_memory_space_constraint(array, pltpu.HBM)
+            for array in (shrink_weight, key_weight, value_weight)
+        ),
         query,
-        in_specs=[whole] * 7 + [hbm] + [whole] * 3,
-        out_specs=(whole,) * 6,
+        in_specs=[whole] * 7 + [hbm] * 3 + [whole],
+        out_specs=(whole,) * 8,
         scratch_shapes=[
             vmem(3, 6, cols + 16, LANES),
             vmem(rows, cols, width),
             *work,
-            pltpu.SemaphoreType.DMA((HID // width,)),
+            pltpu.VMEM(value_weight.shape, bf16),
+            pltpu.SemaphoreType.DMA((6,)),
         ],
     )
     block_out, part = call(

time: 71.9 us -> 71.5 us (level)
  blocking collectives: 48.4 us -> 47.5 us
    all_to_all x3, blocking collectives: 48.4 us -> 47.5 us  [everyone(): lax.all_to_all(part, ('row', 'col'), 0, 0, axis_index_groups=groups, tile...]
  transfers between devices with their start and end apart: 4 -> 4, of which waited for: 1 -> 0; matrix products, arithmetic and copies ran while one was open for 0% -> 0% of each run, Pallas kernels for 5% -> 6%
where the time goes in v5:
time: 71.5 us; the launch traced here: 71.1 us
  blocking collectives  47.5 us (66%)
  starting transfers between devices  12.8 us (18%)
  Pallas kernels  9.75 us (14%)
  between operations  0.83 us (1%)
    all_to_all x3, blocking collectives, everyone(): lax.all_to_all(part, ('row', 'col'), 0, 0, axis_index_groups=groups, tile...  47.5 us
    pallas_call x7, Pallas kernels, call(): pl.pallas_call(kernel, out_shape=out_shape, name=name, **more, **params())  9.75 us
    ppermute x2, starting transfers between devices, swapped(): lax.ppermute(near, axis, inner)  7.67 us
    ppermute x2, starting transfers between devices, swapped(): lax.ppermute(far, axis, outer)  5.17 us
  transfers between devices with their start and end apart: 4, of which 0 were waited for; matrix products, arithmetic and copies ran while one was open for 0% of the time, Pallas kernels for 6%

profile of v5, /device:TPU:1, one launch (start us, length us, event | category | flops | bytes accessed | tf_op | source)
XLA Modules:
  0.0 71.1 jit_solution(12543331977523798777)
XLA Ops:
  0.6 1.0 %fetch_cells.1 = (bf16[8,32,384]{2,1,0:T(8,128)(2,1)S(1)}, f32[7,7,384]{2,1,0:T(8,128)S(1)}, f32[384]{0:T(512)S(1)}, bf16[3,32,384]{2,1,0:T(8,128)(2,1)S(1)}, bf...) custom-call(bf16[8,32,384]{2,1,0:T(8,128)(2,1)} %x_hbm.1, ...), custom_call_target="tpu_custom_call" | custom-call | flops 1000000 | bytes 1000000 | tf_op jit(solution)/shard_map/fetch_cells/pallas_call | solution.py:449
  1.7 4.5 %collective-permute-start.1 = (bf16[3,32,384]{2,1,0:T(8,128)(2,1)S(1)}, bf16[3,32,384]{2,1,0:T(8,128)(2,1)S(1)}, u32[]{:S(2)}, u32[]{:S(2)}) collective-permute-start(bf16[3,32,384]{2,1,0:T(8,128)(2,1)S(1)} %get-tuple-element.37), channel_id=1, source_target_pairs={{8,16},{16,8},{24,32},{32,24},{40,48},{48,40},{56,64},{64,56},{72,... | collective-permute-start | bytes 221192 | tf_op jit(solution)/shard_map/ppermute | solution.py:483
  6.2 4.9 %collective-permute-start = (bf16[3,32,384]{2,1,0:T(8,128)(2,1)S(1)}, bf16[3,32,384]{2,1,0:T(8,128)(2,1)S(1)}, u32[]{:S(2)}, u32[]{:S(2)}) collective-permute-start(bf16[3,32,384]{2,1,0:T(8,128)(2,1)S(1)} %get-tuple-element.36), channel_id=1, source_target_pairs={{0,8},{8,0},{16,24},{24,16},{32,40},{40,32},{48,56},{56,48},{64,72... | collective-permute-start | bytes 221192 | tf_op jit(solution)/shard_map/ppermute | solution.py:483
  11.1 1.4 %own_cells.1 = (f32[8,32,384]{2,1,0:T(8,128)S(1)}, bf16[384,1536]{1,0:T(8,128)(2,1)S(1)}, bf16[64,384]{1,0:T(8,128)(2,1)S(1)}, f32[16,384]{1,0:T(8,128)S(1)}) custom-call(bf16[8,32,384]{2,1,0:T(8,128)(2,1)S(1)} %get-tuple-element.31.x_ref, f32[7,7,384]{2,1,0:T(8,128)S(1)} %get-tuple-element.32.weight_ref, f32[384]{0:T(512)S(1)} %get-tuple-element.33.bias_ref, ...), custom_call_target="tpu_custom_call" | custom-call | flops 1000000 | bytes 1000000 | tf_op jit(solution)/shard_map/own_cells/pallas_call | solution.py:449
  12.6 0.0 collective-permute-done.1
  12.6 0.0 collective-permute-done
  12.7 0.1 broadcast_select_fusion.4
  12.7 0.7 collective-permute-start.3
  13.4 2.7 %collective-permute-start.2 = (bf16[14,3,384]{2,1,0:T(4,128)(2,1)S(1)}, bf16[14,3,384]{2,1,0:T(4,128)(2,1)S(1)}, u32[]{:S(2)}, u32[]{:S(2)}) collective-permute-start(bf16[14,3,384]{2,1,0:T(4,128)(2,1)S(1)} %get-tuple-element.60), channel_id=1, source_target_pairs={{0,1},{1,0},{2,3},{3,2},{4,5},{5,4},{6,7},{7,6},{8,9},{9,8},{10,11... | collective-permute-start | bytes 96776 | tf_op jit(solution)/shard_map/ppermute | solution.py:483
  16.2 0.0 copy-start.1
  16.2 2.9 %inner_cells.1 = (f32[8,16,384]{2,1,0:T(8,128)S(1)}, bf16[8,16,384]{2,1,0:T(8,128)(2,1)S(1)}, bf16[128,384]{1,0:T(8,128)(2,1)S(1)}, bf16[384,128]{1,0:T(8,128)(2...) custom-call(f32[8,32,384]{2,1,0:T(8,128)S(1)} %get-tuple-element.35., ...), custom_call_target="tpu_custom_call" | custom-call | flops 1000000 | bytes 1000000 | tf_op jit(solution)/shard_map/inner_cells/pallas_call | solution.py:449
  19.1 0.0 collective-permute-done.3
  19.1 0.0 collective-permute-done.2
  19.1 0.0 copy-done.1
  19.1 0.0 copy-start
  19.1 0.0 copy-start.2
  19.2 2.6 %outer_cells.1 = (bf16[8,32,384]{2,1,0:T(8,128)(2,1)}, bf16[2,64,256]{2,1,0:T(8,128)(2,1)S(1)}) custom-call(s32[1,4]{1,0:T(1,128)S(1)} %copy-done.1, f32[8,16,384]{2,1,0:T(8,128)S(1)} %get-tuple-element.41.acc_in, bf16[14,3,384]{2,1,0:T(4,128)(2,1)S(1)} %get-tuple-element.58.left_ref, bf16[14,3,384]{2,1,0:T(4,128)(2,1)S(1)} %get-tuple-element.57.right_ref, ...), custom_call_target="tpu_custom_call" | custom-call | flops 1000000 | bytes 1000000 | tf_op jit(solution)/shard_map/outer_cells/pallas_call | solution.py:449
  21.8 13.3 %all_to_all.15.parts_ref = bf16[16,8,256]{2,1,0:T(8,128)(2,1)S(1)} all-to-all(bf16[16,8,256]{2,1,0:T(8,128)(2,1)S(1)} %bitcast.2), channel_id=1, replica_groups={{0,8,16,24,32,40,48,56,64,72,80,88,96,104,112,120},{1,9,17,25,33,41,49,..., dimensions={0} | all-to-all | bytes 131072 | tf_op jit(solution)/shard_map/all_to_all | solution.py:445
  35.1 0.3 merge_first.1
  35.4 23.8 %all_to_all.16.parts_ref = bf16[32,8,256]{2,1,0:T(8,128)(2,1)S(1)} all-to-all(bf16[32,8,256]{2,1,0:T(8,128)(2,1)S(1)} %merge_first.1), channel_id=1, replica_groups={{0,1,2,3,4,5,6,7,128,129,130,131,132,133,134,135,256,257,258,259,260,26..., dimensions={0} | all-to-all | bytes 262144 | tf_op jit(solution)/shard_map/all_to_all | solution.py:445
  59.2 0.3 merge_second.1
  59.5 10.4 %all_to_all.17.parts_ref = bf16[16,8,256]{2,1,0:T(8,128)(2,1)S(1)} all-to-all(bf16[16,8,256]{2,1,0:T(8,128)(2,1)S(1)} %merge_second.1), channel_id=1, replica_groups={{0,8,16,24,32,40,48,56,64,72,80,88,96,104,112,120},{1,9,17,25,33,41,49,..., dimensions={0} | all-to-all | bytes 131072 | tf_op jit(solution)/shard_map/all_to_all | solution.py:445
  69.9 0.0 copy-done
  69.9 0.0 copy-done.2
  69.9 1.2 %pool.1 = (f32[64,384]{1,0:T(8,128)}, f32[1]{0:T(128)}) custom-call(bf16[16,8,256]{2,1,0:T(8,128)(2,1)S(1)} %all_to_all.17.parts_ref, f32[16,384]{1,0:T(8,128)S(1)} %bitcast.3, s32[16]{0:T(128)S(1)} %copy-done.2), custom_call_target="tpu_custom_call" | custom-call | flops 1000000 | bytes 1000000 | tf_op jit(solution)/shard_map/pool/pallas_call | solution.py:449
  (3 shorter events, 0.1 us)
Async XLA Ops:
  1.7 10.9 %collective-permute-start.1 = (bf16[3,32,384]{2,1,0:T(8,128)(2,1)S(1)}, bf16[3,32,384]{2,1,0:T(8,128)(2,1)S(1)}, u32[]{:S(2)}, u32[]{:S(2)}) collective-permute-start(bf16[3,32,384]{2,1,0:T(8,128)(2,1)S(1)} %get-tuple-element.37), channel_id=1, source_target_pairs={{8,16},{16,8},{24,32},{32,24},{40,48},{48,40},{56,64},{64,56},{72,... | collective-permute-start | bytes 221192 | tf_op jit(solution)/shard_map/ppermute | solution.py:483
  6.2 6.4 %collective-permute-start = (bf16[3,32,384]{2,1,0:T(8,128)(2,1)S(1)}, bf16[3,32,384]{2,1,0:T(8,128)(2,1)S(1)}, u32[]{:S(2)}, u32[]{:S(2)}) collective-permute-start(bf16[3,32,384]{2,1,0:T(8,128)(2,1)S(1)} %get-tuple-element.36), channel_id=1, source_target_pairs={{0,8},{8,0},{16,24},{24,16},{32,40},{40,32},{48,56},{56,48},{64,72... | collective-permute-start | bytes 221192 | tf_op jit(solution)/shard_map/ppermute | solution.py:483
  12.7 6.3 %collective-permute-start.3 = (bf16[14,3,384]{2,1,0:T(4,128)(2,1)S(1)}, bf16[14,3,384]{2,1,0:T(4,128)(2,1)S(1)}, u32[]{:S(2)}, u32[]{:S(2)}) collective-permute-start(bf16[14,3,384]{2,1,0:T(4,128)(2,1)S(1)} %get-tuple-element.59), channel_id=1, source_target_pairs={{1,2},{2,1},{3,4},{4,3},{5,6},{6,5},{9,10},{10,9},{11,12},{12,11},... | collective-permute-start | bytes 96776 | tf_op jit(solution)/shard_map/ppermute | solution.py:483
  13.4 5.6 %collective-permute-start.2 = (bf16[14,3,384]{2,1,0:T(4,128)(2,1)S(1)}, bf16[14,3,384]{2,1,0:T(4,128)(2,1)S(1)}, u32[]{:S(2)}, u32[]{:S(2)}) collective-permute-start(bf16[14,3,384]{2,1,0:T(4,128)(2,1)S(1)} %get-tuple-element.60), channel_id=1, source_target_pairs={{0,1},{1,0},{2,3},{3,2},{4,5},{5,4},{6,7},{7,6},{8,9},{9,8},{10,11... | collective-permute-start | bytes 96776 | tf_op jit(solution)/shard_map/ppermute | solution.py:483
  16.2 3.0 %copy-start.1 = (s32[1,4]{1,0:T(1,128)S(1)}, s32[1,4]{1,0:T(1,128)}, u32[]{:S(2)}) copy-start(s32[1,4]{1,0:T(1,128)} %tissue_ref.1) | copy-start | bytes 52
  19.1 50.8 %copy-start = (f32[384,16]{0,1:T(8,128)S(1)}, f32[384,16]{0,1:T(8,128)}, u32[]{:S(2)}) copy-start(f32[384,16]{0,1:T(8,128)} %param.29) | copy-start | bytes 73732
  19.1 50.8 %copy-start.2 = (s32[16]{0:T(128)S(1)}, s32[16]{0:T(128)}, u32[]{:S(2)}) copy-start(s32[16]{0:T(128)} %label_ref.1) | copy-start | bytes 196

commit v6 on v5

--- a/solution.py
+++ b/solution.py
@@ -59,7 +59,6 @@
     x_ref,
     weight_ref,
     bias_ref,
-    expand_hbm,
     query_hbm,
     gain_hbm,
     norm_bias_hbm,
@@ -67,7 +66,6 @@
     scale_hbm,
     expand_bias_hbm,
     acc_ref,
-    expand_ref,
     query_ref,
     rows_ref,
     wide,
@@ -85,10 +83,6 @@
         (scale_hbm, scale_ref),
         (expand_bias_hbm, expand_bias_ref),
         (query_hbm, query_ref),
-        *(
-            (expand_hbm.at[k : k + LANES], expand_ref.at[k : k + LANES])
-            for k in range(0, WIDTH, LANES)
-        ),
     )
     copies = [pltpu.make_async_copy(s, d, sems.at[k]) for k, (s, d) in enumerate(pairs)]
     for copy in copies:
@@ -216,7 +210,7 @@
     weight_ref,
     x_ref,
     lines_ref,
-    expand_ref,
+    expand_hbm,
     shrink_hbm,
     key_hbm,
     value_hbm,
@@ -225,6 +219,7 @@
     block_ref,
     keys_ref,
     values_ref,
+    expand_ref,
     shrink_ref,
     key_ref,
     turned_ref,
@@ -248,11 +243,18 @@
         pltpu.make_async_copy(value_hbm, value_ref, sems.at[4]),
         pltpu.make_async_copy(key_hbm, key_ref, sems.at[5]),
     ]
-    for copy in copies + late:
+    early = [
+        pltpu.make_async_copy(
+            expand_hbm.at[k * LANES : (k + 1) * LANES],
+            expand_ref.at[k * LANES : (k + 1) * LANES],
+            sems.at[6 + k],
+        )
+        for k in range(WIDTH // LANES)
+    ]
+    for copy in late[:1] + early + copies + late[1:]:
         copy.start()
     halo_rows(acc_in, low_ref, high_ref, weight_ref, acc_ref, wide)
-    for copy in late:
-        copy.wait()
+    late[0].wait()
     turned_ref[...] = value_ref[...].astype(jnp.float32).T.astype(jnp.bfloat16)
     query = query_ref[...].astype(jnp.float32)
     query = jnp.concatenate([query, query], axis=0).T
@@ -264,6 +266,8 @@
         ).astype(jnp.bfloat16)
     sides_ref[:, 0:8, :] = acc_ref[:, 0:8, :]
     sides_ref[:, 8:16, :] = acc_ref[:, CELLS_C - 8 : CELLS_C, :]
+    for copy in early:
+        copy.wait()
     block = block_of(
         lambda i: acc_ref[i, 8 : 8 + HALF, :],
         x_ref[:, 8 : 8 + HALF, :],
@@ -275,6 +279,7 @@
         copies,
     )
     block_ref[...] = block.reshape(CELLS_R, HALF, WIDTH)
+    late[1].wait()
     keys_ref[...] = keys_of(block, key_ref)
     values_ref[...] = values_of(block, turned_ref)
 
@@ -530,11 +535,10 @@
         scratch_shapes=[pltpu.SemaphoreType.DMA((3,))],
     )
     low, high = swapped(near, far, "row")
-    acc, expand, query, lines = call(
+    acc, query, lines = call(
         own_kernel,
         (
             shaped((rows, cols, width), f32),
-            shaped(expand_weight.shape, bf16),
             shaped(queries.shape, bf16),
             shaped((16, width), f32),
         ),
@@ -545,7 +549,6 @@
         *(
             pltpu.with_memory_space_constraint(array, pltpu.HBM)
             for array in (
-                expand_weight,
                 queries,
                 norm_gain,
                 norm_bias,
@@ -554,13 +557,13 @@
                 expand_bias,
             )
         ),
-        in_specs=[whole] * 3 + [hbm] * 7,
-        out_specs=(whole,) * 4,
+        in_specs=[whole] * 3 + [hbm] * 6,
+        out_specs=(whole,) * 3,
         scratch_shapes=[
             vmem(3 * cols // 8, rows, 24, LANES),
             *(vmem(width) for _ in range(4)),
             vmem(HID),
-            pltpu.SemaphoreType.DMA((9,)),
+            pltpu.SemaphoreType.DMA((6,)),
         ],
     )
     first, last, acc = lax.optimization_barrier((first, last, acc))
@@ -571,13 +574,14 @@
     )
     count = rows * HALF
     work = [pltpu.VMEM((count, width), bf16), pltpu.VMEM((count, HID), bf16)]
-    sides, inner, keys, values, shrink, key, turned, big = call(
+    sides, inner, keys, values, expand, shrink, key, turned, big = call(
         inner_kernel,
         (
             shaped((rows, HALF, width), f32),
             shaped((rows, HALF, width), bf16),
             shaped((count, width), bf16),
             shaped((width, count), bf16),
+            shaped(expand_weight.shape, bf16),
             shaped(shrink_weight.shape, bf16),
             shaped(key_weight.shape, bf16),
             shaped(value_weight.shape, bf16),
@@ -590,20 +594,19 @@
         taps_,
         cells,
         lines,
-        expand,
         *(
             pltpu.with_memory_space_constraint(array, pltpu.HBM)
-            for array in (shrink_weight, key_weight, value_weight)
+            for array in (expand_weight, shrink_weight, key_weight, value_weight)
         ),
         query,
-        in_specs=[whole] * 7 + [hbm] * 3 + [whole],
-        out_specs=(whole,) * 8,
+        in_specs=[whole] * 6 + [hbm] * 4 + [whole],
+        out_specs=(whole,) * 9,
         scratch_shapes=[
             vmem(3, 6, cols + 16, LANES),
             vmem(rows, cols, width),
             *work,
             pltpu.VMEM(value_weight.shape, bf16),
-            pltpu.SemaphoreType.DMA((6,)),
+            pltpu.SemaphoreType.DMA((9,)),
         ],
     )
     block_out, part = call(

time: 71.5 us -> 71.4 us (level)
  no operation moved by 1% of the time
where the time goes in v6:
time: 71.4 us; the launch traced here: 71.1 us
  blocking collectives  47.6 us (67%)
  starting transfers between devices  12.8 us (18%)
  Pallas kernels  9.59 us (13%)
  between operations  0.83 us (1%)
    all_to_all x3, blocking collectives, everyone(): lax.all_to_all(part, ('row', 'col'), 0, 0, axis_index_groups=groups, tile...  47.6 us
    pallas_call x7, Pallas kernels, call(): pl.pallas_call(kernel, out_shape=out_shape, name=name, **more, **params())  9.59 us
    ppermute x2, starting transfers between devices, swapped(): lax.ppermute(near, axis, inner)  7.67 us
    ppermute x2, starting transfers between devices, swapped(): lax.ppermute(far, axis, outer)  5.17 us
  transfers between devices with their start and end apart: 4, of which 0 were waited for; matrix products, arithmetic and copies ran while one was open for 0% of the time, Pallas kernels for 6%

profile of v6, /device:TPU:1, one launch (start us, length us, event | category | flops | bytes accessed | tf_op | source)
XLA Modules:
  0.0 71.1 jit_solution(5276660225746826512)
XLA Ops:
  0.6 1.0 %fetch_cells.1 = (bf16[8,32,384]{2,1,0:T(8,128)(2,1)S(1)}, f32[7,7,384]{2,1,0:T(8,128)S(1)}, f32[384]{0:T(512)S(1)}, bf16[3,32,384]{2,1,0:T(8,128)(2,1)S(1)}, bf...) custom-call(bf16[8,32,384]{2,1,0:T(8,128)(2,1)} %x_hbm.1, ...), custom_call_target="tpu_custom_call" | custom-call | flops 1000000 | bytes 1000000 | tf_op jit(solution)/shard_map/fetch_cells/pallas_call | solution.py:454
  1.7 4.5 %collective-permute-start.1 = (bf16[3,32,384]{2,1,0:T(8,128)(2,1)S(1)}, bf16[3,32,384]{2,1,0:T(8,128)(2,1)S(1)}, u32[]{:S(2)}, u32[]{:S(2)}) collective-permute-start(bf16[3,32,384]{2,1,0:T(8,128)(2,1)S(1)} %get-tuple-element.37), channel_id=1, source_target_pairs={{8,16},{16,8},{24,32},{32,24},{40,48},{48,40},{56,64},{64,56},{72,... | collective-permute-start | bytes 221192 | tf_op jit(solution)/shard_map/ppermute | solution.py:488
  6.2 4.9 %collective-permute-start = (bf16[3,32,384]{2,1,0:T(8,128)(2,1)S(1)}, bf16[3,32,384]{2,1,0:T(8,128)(2,1)S(1)}, u32[]{:S(2)}, u32[]{:S(2)}) collective-permute-start(bf16[3,32,384]{2,1,0:T(8,128)(2,1)S(1)} %get-tuple-element.36), channel_id=1, source_target_pairs={{0,8},{8,0},{16,24},{24,16},{32,40},{40,32},{48,56},{56,48},{64,72... | collective-permute-start | bytes 221192 | tf_op jit(solution)/shard_map/ppermute | solution.py:488
  11.1 1.4 %own_cells.1 = (f32[8,32,384]{2,1,0:T(8,128)S(1)}, bf16[64,384]{1,0:T(8,128)(2,1)S(1)}, f32[16,384]{1,0:T(8,128)S(1)}) custom-call(bf16[8,32,384]{2,1,0:T(8,128)(2,1)S(1)} %get-tuple-element.31.x_ref, f32[7,7,384]{2,1,0:T(8,128)S(1)} %get-tuple-element.32.weight_ref, f32[384]{0:T(512)S(1)} %get-tuple-element.33.bias_ref, bf16[64,384]{1,0:T(8,128)(2,1)} %query_hbm.1, ...), custom_call_target="tpu_custom_call" | custom-call | flops 1000000 | bytes 1000000 | tf_op jit(solution)/shard_map/own_cells/pallas_call | solution.py:454
  12.6 0.0 collective-permute-done.1
  12.6 0.0 collective-permute-done
  12.6 0.1 broadcast_select_fusion.4
  12.7 0.7 collective-permute-start.3
  13.4 2.7 %collective-permute-start.2 = (bf16[14,3,384]{2,1,0:T(4,128)(2,1)S(1)}, bf16[14,3,384]{2,1,0:T(4,128)(2,1)S(1)}, u32[]{:S(2)}, u32[]{:S(2)}) collective-permute-start(bf16[14,3,384]{2,1,0:T(4,128)(2,1)S(1)} %get-tuple-element.60), channel_id=1, source_target_pairs={{0,1},{1,0},{2,3},{3,2},{4,5},{5,4},{6,7},{7,6},{8,9},{9,8},{10,11... | collective-permute-start | bytes 96776 | tf_op jit(solution)/shard_map/ppermute | solution.py:488
  16.1 0.0 copy-start.1
  16.1 2.7 %inner_cells.1 = (f32[8,16,384]{2,1,0:T(8,128)S(1)}, bf16[8,16,384]{2,1,0:T(8,128)(2,1)S(1)}, bf16[128,384]{1,0:T(8,128)(2,1)S(1)}, bf16[384,128]{1,0:T(8,128)(2...) custom-call(f32[8,32,384]{2,1,0:T(8,128)S(1)} %get-tuple-element.35., ...), custom_call_target="tpu_custom_call" | custom-call | flops 1000000 | bytes 1000000 | tf_op jit(solution)/shard_map/inner_cells/pallas_call | solution.py:454
  18.9 0.0 collective-permute-done.3
  18.9 0.0 collective-permute-done.2
  18.9 0.0 copy-done.1
  19.0 0.0 copy-start
  19.0 0.0 copy-start.2
  19.0 2.6 %outer_cells.1 = (bf16[8,32,384]{2,1,0:T(8,128)(2,1)}, bf16[2,64,256]{2,1,0:T(8,128)(2,1)S(1)}) custom-call(s32[1,4]{1,0:T(1,128)S(1)} %copy-done.1, f32[8,16,384]{2,1,0:T(8,128)S(1)} %get-tuple-element.40.acc_in, bf16[14,3,384]{2,1,0:T(4,128)(2,1)S(1)} %get-tuple-element.58.left_ref, bf16[14,3,384]{2,1,0:T(4,128)(2,1)S(1)} %get-tuple-element.57.right_ref, ...), custom_call_target="tpu_custom_call" | custom-call | flops 1000000 | bytes 1000000 | tf_op jit(solution)/shard_map/outer_cells/pallas_call | solution.py:454
  21.6 13.3 %all_to_all.15.parts_ref = bf16[16,8,256]{2,1,0:T(8,128)(2,1)S(1)} all-to-all(bf16[16,8,256]{2,1,0:T(8,128)(2,1)S(1)} %bitcast.2), channel_id=1, replica_groups={{0,8,16,24,32,40,48,56,64,72,80,88,96,104,112,120},{1,9,17,25,33,41,49,..., dimensions={0} | all-to-all | bytes 131072 | tf_op jit(solution)/shard_map/all_to_all | solution.py:450
  35.0 0.3 merge_first.1
  35.3 23.9 %all_to_all.16.parts_ref = bf16[32,8,256]{2,1,0:T(8,128)(2,1)S(1)} all-to-all(bf16[32,8,256]{2,1,0:T(8,128)(2,1)S(1)} %merge_first.1), channel_id=1, replica_groups={{0,1,2,3,4,5,6,7,128,129,130,131,132,133,134,135,256,257,258,259,260,26..., dimensions={0} | all-to-all | bytes 262144 | tf_op jit(solution)/shard_map/all_to_all | solution.py:450
  59.2 0.3 merge_second.1
  59.5 10.4 %all_to_all.17.parts_ref = bf16[16,8,256]{2,1,0:T(8,128)(2,1)S(1)} all-to-all(bf16[16,8,256]{2,1,0:T(8,128)(2,1)S(1)} %merge_second.1), channel_id=1, replica_groups={{0,8,16,24,32,40,48,56,64,72,80,88,96,104,112,120},{1,9,17,25,33,41,49,..., dimensions={0} | all-to-all | bytes 131072 | tf_op jit(solution)/shard_map/all_to_all | solution.py:450
  69.9 0.0 copy-done
  69.9 0.0 copy-done.2
  69.9 1.2 %pool.1 = (f32[64,384]{1,0:T(8,128)}, f32[1]{0:T(128)}) custom-call(bf16[16,8,256]{2,1,0:T(8,128)(2,1)S(1)} %all_to_all.17.parts_ref, f32[16,384]{1,0:T(8,128)S(1)} %bitcast.3, s32[16]{0:T(128)S(1)} %copy-done.2), custom_call_target="tpu_custom_call" | custom-call | flops 1000000 | bytes 1000000 | tf_op jit(solution)/shard_map/pool/pallas_call | solution.py:454
  (3 shorter events, 0.1 us)
Async XLA Ops:
  1.7 10.9 %collective-permute-start.1 = (bf16[3,32,384]{2,1,0:T(8,128)(2,1)S(1)}, bf16[3,32,384]{2,1,0:T(8,128)(2,1)S(1)}, u32[]{:S(2)}, u32[]{:S(2)}) collective-permute-start(bf16[3,32,384]{2,1,0:T(8,128)(2,1)S(1)} %get-tuple-element.37), channel_id=1, source_target_pairs={{8,16},{16,8},{24,32},{32,24},{40,48},{48,40},{56,64},{64,56},{72,... | collective-permute-start | bytes 221192 | tf_op jit(solution)/shard_map/ppermute | solution.py:488
  6.2 6.4 %collective-permute-start = (bf16[3,32,384]{2,1,0:T(8,128)(2,1)S(1)}, bf16[3,32,384]{2,1,0:T(8,128)(2,1)S(1)}, u32[]{:S(2)}, u32[]{:S(2)}) collective-permute-start(bf16[3,32,384]{2,1,0:T(8,128)(2,1)S(1)} %get-tuple-element.36), channel_id=1, source_target_pairs={{0,8},{8,0},{16,24},{24,16},{32,40},{40,32},{48,56},{56,48},{64,72... | collective-permute-start | bytes 221192 | tf_op jit(solution)/shard_map/ppermute | solution.py:488
  12.7 6.2 %collective-permute-start.3 = (bf16[14,3,384]{2,1,0:T(4,128)(2,1)S(1)}, bf16[14,3,384]{2,1,0:T(4,128)(2,1)S(1)}, u32[]{:S(2)}, u32[]{:S(2)}) collective-permute-start(bf16[14,3,384]{2,1,0:T(4,128)(2,1)S(1)} %get-tuple-element.59), channel_id=1, source_target_pairs={{1,2},{2,1},{3,4},{4,3},{5,6},{6,5},{9,10},{10,9},{11,12},{12,11},... | collective-permute-start | bytes 96776 | tf_op jit(solution)/shard_map/ppermute | solution.py:488
  13.4 5.5 %collective-permute-start.2 = (bf16[14,3,384]{2,1,0:T(4,128)(2,1)S(1)}, bf16[14,3,384]{2,1,0:T(4,128)(2,1)S(1)}, u32[]{:S(2)}, u32[]{:S(2)}) collective-permute-start(bf16[14,3,384]{2,1,0:T(4,128)(2,1)S(1)} %get-tuple-element.60), channel_id=1, source_target_pairs={{0,1},{1,0},{2,3},{3,2},{4,5},{5,4},{6,7},{7,6},{8,9},{9,8},{10,11... | collective-permute-start | bytes 96776 | tf_op jit(solution)/shard_map/ppermute | solution.py:488
  16.1 2.8 %copy-start.1 = (s32[1,4]{1,0:T(1,128)S(1)}, s32[1,4]{1,0:T(1,128)}, u32[]{:S(2)}) copy-start(s32[1,4]{1,0:T(1,128)} %tissue_ref.1) | copy-start | bytes 52
  19.0 50.9 %copy-start = (f32[384,16]{0,1:T(8,128)S(1)}, f32[384,16]{0,1:T(8,128)}, u32[]{:S(2)}) copy-start(f32[384,16]{0,1:T(8,128)} %param.29) | copy-start | bytes 73732
  19.0 50.9 %copy-start.2 = (s32[16]{0:T(128)S(1)}, s32[16]{0:T(128)}, u32[]{:S(2)}) copy-start(s32[16]{0:T(128)} %label_ref.1) | copy-start | bytes 196
